TPU v7x, 32 devices: a whole 2x2x4 slice. The times are simulated.
32 devices in a mesh: dp: 4 (over y, core), fsdp: 8 (over z, x).
Axes of the slice: x: 2, y: 2, z: 4, core: 2. Of those that a mesh axis runs over, the one named last changes fastest.
Arguments:
- tokens: bfloat16 [32768, 768], P(('dp', 'fsdp')), may hold values from -6 to 6
- doc_start: int32 [256], P(('dp', 'fsdp')), may hold values from 0 to 7, as said below
- attn_gain: bfloat16 [768], P(('dp', 'fsdp')), may hold values from 0.5 to 1.5
- attn_bias: bfloat16 [768], P(('dp', 'fsdp')), may hold values from -1.5 to 1.5
- w_query: bfloat16 [768, 768], P(('dp', 'fsdp')), may hold values from -0.21875 to 0.21875
- w_key: bfloat16 [768, 768], P(('dp', 'fsdp')), may hold values from -0.21875 to 0.21875
- w_value: bfloat16 [768, 768], P(('dp', 'fsdp')), may hold values from -0.21875 to 0.21875
- shift_taps: bfloat16 [768, 64], P(('dp', 'fsdp')), may hold values from -0.75 to 0.75
- log_step: bfloat16 [768], P(('dp', 'fsdp')), may hold values from -6.875 to -2.296875
- state_out: bfloat16 [768, 64], P(('dp', 'fsdp')), may hold values from -5 to 5
- log_rate: bfloat16 [768, 64], P(('dp', 'fsdp')), may hold values from -0.69921875 to 4.1875
- w_output: bfloat16 [768, 768], P(('dp', 'fsdp')), may hold values from -0.21875 to 0.21875
- mlp_gain: bfloat16 [768], P(('dp', 'fsdp')), may hold values from 0.5 to 1.5
- mlp_bias: bfloat16 [768], P(('dp', 'fsdp')), may hold values from -1.5 to 1.5
- w_up: bfloat16 [768, 3072], P(('dp', 'fsdp')), may hold values from -0.21875 to 0.21875
- w_down: bfloat16 [3072, 768], P(('dp', 'fsdp')), may hold values from -0.109375 to 0.109375
- cotangent: bfloat16 [32768, 768], P(('dp', 'fsdp')), may hold values from -6 to 6
Outputs:
- layer_out: bfloat16 [32768, 768], P(('dp', 'fsdp'))
- tokens_grad: float32 [32768, 768], P(('dp', 'fsdp'))
- attn_gain_grad: float32 [768], P(('dp', 'fsdp'))
- attn_bias_grad: float32 [768], P(('dp', 'fsdp'))
- query_grad: float32 [768, 768], P(('dp', 'fsdp'))
- key_grad: float32 [768, 768], P(('dp', 'fsdp'))
- value_grad: float32 [768, 768], P(('dp', 'fsdp'))
- taps_grad: float32 [768, 64], P(('dp', 'fsdp'))
- step_grad: float32 [768], P(('dp', 'fsdp'))
- state_grad: float32 [768, 64], P(('dp', 'fsdp'))
- rate_grad: float32 [768, 64], P(('dp', 'fsdp'))
- output_grad: float32 [768, 768], P(('dp', 'fsdp'))
- mlp_gain_grad: float32 [768], P(('dp', 'fsdp'))
- mlp_bias_grad: float32 [768], P(('dp', 'fsdp'))
- up_grad: float32 [768, 3072], P(('dp', 'fsdp'))
- down_grad: float32 [3072, 768], P(('dp', 'fsdp'))
Inputs may be any that keep to these rules, and one draw needn't show every extreme that they name: `doc_start`: each device's 8 consecutive entries split its blocks into whole sequences of whole blocks: entry i is the first block of the sequence holding block i, so entries never fall within a sequence and equal i at a sequence's start. The first device holds one sequence of 8 blocks and the second 8 sequences of one block.
All inputs are finite; a program needn't handle non-finite values.
Results may differ from a plain program's by a relative error of at most 0.011.
Values may be sent and summed in bfloat16 or wider, within the bound.
A program may use at most 256 MiB of HBM per device.

v0:
```python
from functools import partial
import math

import jax
import jax.numpy as jnp
from jax import lax
from jax.sharding import PartitionSpec as P


def make_kernel(log_step, state_out, log_rate, blocks, length):
    step_size = jnp.exp(log_step)[:, None]
    decay_rate = step_size * jnp.exp(log_rate)
    weight = state_out * step_size

    def one_block(block_first):
        places = block_first + jnp.arange(length).astype(log_step.dtype)
        decays = jnp.exp(-decay_rate[None, :, :] * places[:, None, None])
        return jnp.sum(decays * weight[None, :, :], axis=2)

    block_starts = (jnp.arange(blocks) * length).astype(log_step.dtype)
    return lax.map(jax.checkpoint(one_block), block_starts).reshape(blocks * length, -1)


def dft_tables(block_len):
    period = 2 * block_len
    freqs = jnp.arange(block_len + 1)
    times = jnp.arange(period)
    turns = freqs[:, None] * times[None, :] % period
    angles = turns.astype(jnp.float32) * (2.0 * math.pi / period)
    cosine_table = jnp.cos(angles)
    sine_table = jnp.sin(angles)
    edge = (freqs == 0) | (freqs == block_len)
    weights = (jnp.where(edge, 1.0, 2.0) / period).astype(jnp.float32)[:, None]
    return (cosine_table, sine_table, cosine_table * weights, sine_table * weights)


def to_spectrum(signal, cosine_table, sine_table):
    real_part = jnp.einsum("ft,ntc->nfc", cosine_table, signal, precision=lax.Precision.HIGH)
    imag_part = -jnp.einsum("ft,ntc->nfc", sine_table, signal, precision=lax.Precision.HIGH)
    return (real_part, imag_part)


def to_time(real_part, imag_part, inverse_cosine, inverse_sine):
    cos_terms = jnp.einsum("ft,nfc->ntc", inverse_cosine, real_part, precision=lax.Precision.HIGH)
    sin_terms = jnp.einsum("ft,nfc->ntc", inverse_sine, imag_part, precision=lax.Precision.HIGH)
    return cos_terms - sin_terms


def kernel_segments(kernel, block_count):
    block_len = kernel.shape[0] // block_count
    feature_width = kernel.shape[1]
    padded = jnp.concatenate([jnp.zeros((block_len, feature_width), jnp.float32), kernel], axis=0)
    upper = padded[block_len:].reshape(block_count, block_len, feature_width)
    lower = padded[: block_count * block_len].reshape(block_count, block_len, feature_width)
    return jnp.concatenate([upper, lower], axis=1)


def segments_to_kernel(segment_grad):
    block_count = segment_grad.shape[0]
    block_len = segment_grad.shape[1] // 2
    feature_width = segment_grad.shape[2]
    upper_grad = segment_grad[:, :block_len].reshape(block_count * block_len, feature_width)
    lower_grad = segment_grad[1:, block_len:].reshape((block_count - 1) * block_len, feature_width)
    return upper_grad + jnp.concatenate(
        [lower_grad, jnp.zeros((block_len, feature_width), jnp.float32)], axis=0
    )


def mix_forward(kernel_spec, signal_spec, starts):
    kernel_real, kernel_imag = kernel_spec
    signal_real, signal_imag = signal_spec
    block_count = starts.shape[0]
    places = jnp.arange(block_count)

    def add_offset(offset, totals):
        total_real, total_imag = totals
        moved_real = jnp.roll(signal_real, offset, axis=0)
        moved_imag = jnp.roll(signal_imag, offset, axis=0)
        taps_real = lax.dynamic_index_in_dim(kernel_real, offset, 0, keepdims=False)
        taps_imag = lax.dynamic_index_in_dim(kernel_imag, offset, 0, keepdims=False)
        usable = (places - offset >= starts)[:, None, None]
        part_real = taps_real * moved_real - taps_imag * moved_imag
        part_imag = taps_real * moved_imag + taps_imag * moved_real
        return (
            total_real + jnp.where(usable, part_real, 0.0),
            total_imag + jnp.where(usable, part_imag, 0.0),
        )

    empty = jnp.zeros_like(signal_real)
    return lax.fori_loop(0, kernel_real.shape[0], add_offset, (empty, empty))


def mix_backward(kernel_spec, grad_spec, starts):
    kernel_real, kernel_imag = kernel_spec
    grad_real, grad_imag = grad_spec
    block_count = starts.shape[0]
    places = jnp.arange(block_count)

    def add_offset(offset, totals):
        total_real, total_imag = totals
        moved_real = jnp.roll(grad_real, -offset, axis=0)
        moved_imag = jnp.roll(grad_imag, -offset, axis=0)
        taps_real = lax.dynamic_index_in_dim(kernel_real, offset, 0, keepdims=False)
        taps_imag = lax.dynamic_index_in_dim(kernel_imag, offset, 0, keepdims=False)
        usable = jnp.roll(places - offset >= starts, -offset)[:, None, None]
        part_real = taps_real * moved_real + taps_imag * moved_imag
        part_imag = taps_real * moved_imag - taps_imag * moved_real
        return (
            total_real + jnp.where(usable, part_real, 0.0),
            total_imag + jnp.where(usable, part_imag, 0.0),
        )

    empty = jnp.zeros_like(grad_real)
    return lax.fori_loop(0, kernel_real.shape[0], add_offset, (empty, empty))


def mix_kernel(signal_spec, grad_spec, starts, offset_count):
    signal_real, signal_imag = signal_spec
    grad_real, grad_imag = grad_spec
    block_count = starts.shape[0]
    places = jnp.arange(block_count)

    def add_offset(offset, totals):
        total_real, total_imag = totals
        moved_real = jnp.roll(signal_real, offset, axis=0)
        moved_imag = jnp.roll(signal_imag, offset, axis=0)
        usable = (places - offset >= starts)[:, None, None]
        part_real = jnp.sum(
            jnp.where(usable, grad_real * moved_real + grad_imag * moved_imag, 0.0), axis=0
        )
        part_imag = jnp.sum(
            jnp.where(usable, grad_imag * moved_real - grad_real * moved_imag, 0.0), axis=0
        )
        return (
            lax.dynamic_update_index_in_dim(total_real, part_real, offset, 0),
            lax.dynamic_update_index_in_dim(total_imag, part_imag, offset, 0),
        )

    empty = jnp.zeros((offset_count,) + signal_real.shape[1:], jnp.float32)
    return lax.fori_loop(0, offset_count, add_offset, (empty, empty))


def conv_forward(values, kernel_spec, starts, tables):
    (
        fwd_cos_half,
        fwd_sin_half,
        inv_cos_half,
        inv_sin_half,
        fwd_cos_full,
        fwd_sin_full,
        inv_cos_full,
        inv_sin_full,
    ) = tables
    block_count = starts.shape[0]
    blocks = values.reshape(block_count, -1, values.shape[1])
    signal_spec = to_spectrum(blocks, fwd_cos_half, fwd_sin_half)
    mixed_real, mixed_imag = mix_forward(kernel_spec, signal_spec, starts)
    return (
        to_time(mixed_real, mixed_imag, inv_cos_half, inv_sin_half).reshape(values.shape),
        signal_spec,
    )


def conv_backward(grad_values, kernel_spec, signal_spec, starts, tables):
    (
        fwd_cos_half,
        fwd_sin_half,
        inv_cos_half,
        inv_sin_half,
        fwd_cos_full,
        fwd_sin_full,
        inv_cos_full,
        inv_sin_full,
    ) = tables
    block_count = starts.shape[0]
    blocks = grad_values.reshape(block_count, -1, grad_values.shape[1])
    grad_spec = to_spectrum(blocks, fwd_cos_half, fwd_sin_half)
    back_real, back_imag = mix_backward(kernel_spec, grad_spec, starts)
    signal_grad = to_time(back_real, back_imag, inv_cos_half, inv_sin_half).reshape(
        grad_values.shape
    )
    seg_real, seg_imag = mix_kernel(signal_spec, grad_spec, starts, kernel_spec[0].shape[0])
    segment_grad = to_time(seg_real, seg_imag, inv_cos_full, inv_sin_full)
    return (signal_grad, segments_to_kernel(segment_grad))


def norm_parts(values, norm_gain, norm_bias):
    row_mean = jnp.mean(values, axis=-1, keepdims=True)
    centred = values - row_mean
    row_var = jnp.mean(centred * centred, axis=-1, keepdims=True)
    inverse = lax.rsqrt(row_var + 1e-05)
    unit_rows = centred * inverse
    return (
        unit_rows * norm_gain.astype(jnp.float32) + norm_bias.astype(jnp.float32),
        unit_rows,
        inverse,
    )


def norm_back(grad_out, unit_rows, inverse, norm_gain):
    scaled = grad_out * norm_gain.astype(jnp.float32)
    mean_plain = jnp.mean(scaled, axis=-1, keepdims=True)
    mean_unit = jnp.mean(scaled * unit_rows, axis=-1, keepdims=True)
    input_grad = inverse * (scaled - mean_plain - unit_rows * mean_unit)
    return (input_grad, jnp.sum(grad_out * unit_rows, axis=0), jnp.sum(grad_out, axis=0))


def matmul_rows(left, right):
    return jnp.dot(left, right, preferred_element_type=jnp.float32)


def matmul_back(left, right):
    return jnp.einsum("td,cd->tc", left, right, preferred_element_type=jnp.float32)


def matmul_weight(left, right):
    return jnp.einsum("tc,td->cd", left, right, preferred_element_type=jnp.float32)


def shards(
    tokens,
    doc_start,
    attn_gain,
    attn_bias,
    w_query,
    w_key,
    w_value,
    shift_taps,
    log_step,
    state_out,
    log_rate,
    w_output,
    mlp_gain,
    mlp_bias,
    w_up,
    w_down,
    cotangent,
):
    owned = (
        attn_gain,
        attn_bias,
        w_query,
        w_key,
        w_value,
        shift_taps,
        log_step,
        state_out,
        log_rate,
        w_output,
        mlp_gain,
        mlp_bias,
        w_up,
        w_down,
    )
    gathered = (
        lax.all_gather(owned[0], ("dp", "fsdp"), axis=0, tiled=True),
        lax.all_gather(owned[1], ("dp", "fsdp"), axis=0, tiled=True),
        lax.all_gather(owned[2], ("dp", "fsdp"), axis=0, tiled=True),
        lax.all_gather(owned[3], ("dp", "fsdp"), axis=0, tiled=True),
        lax.all_gather(owned[4], ("dp", "fsdp"), axis=0, tiled=True),
        lax.all_gather(owned[5], ("dp", "fsdp"), axis=0, tiled=True),
        lax.all_gather(owned[6], ("dp", "fsdp"), axis=0, tiled=True),
        lax.all_gather(owned[7], ("dp", "fsdp"), axis=0, tiled=True),
        lax.all_gather(owned[8], ("dp", "fsdp"), axis=0, tiled=True),
        lax.all_gather(owned[9], ("dp", "fsdp"), axis=0, tiled=True),
        lax.all_gather(owned[10], ("dp", "fsdp"), axis=0, tiled=True),
        lax.all_gather(owned[11], ("dp", "fsdp"), axis=0, tiled=True),
        lax.all_gather(owned[12], ("dp", "fsdp"), axis=0, tiled=True),
        lax.all_gather(owned[13], ("dp", "fsdp"), axis=0, tiled=True),
    )
    (
        gain_first,
        bias_first,
        query_weight,
        key_weight,
        value_weight,
        taps_weight,
        step_weight,
        state_weight,
        rate_weight,
        output_weight,
        gain_second,
        bias_second,
        up_weight,
        down_weight,
    ) = gathered
    row_total = tokens.shape[0]
    block_count = doc_start.shape[0]
    block_len = row_total // block_count
    tap_count = taps_weight.shape[1]
    fwd_cos, fwd_sin, inv_cos, inv_sin = dft_tables(block_len)
    tables = (
        fwd_cos[:, :block_len],
        fwd_sin[:, :block_len],
        inv_cos[:, :block_len],
        inv_sin[:, :block_len],
        fwd_cos,
        fwd_sin,
        inv_cos,
        inv_sin,
    )
    kernel_fn = partial(make_kernel, blocks=block_count, length=block_len)
    kernel_long, kernel_pull = jax.vjp(
        kernel_fn,
        step_weight.astype(jnp.float32),
        state_weight.astype(jnp.float32),
        rate_weight.astype(jnp.float32),
    )
    kernel_shift = jnp.pad(
        taps_weight.astype(jnp.float32).T, ((0, 2 * block_len - tap_count), (0, 0))
    )
    long_spec = to_spectrum(kernel_segments(kernel_long, block_count), fwd_cos, fwd_sin)
    shift_spec = to_spectrum(kernel_segments(kernel_shift, 2), fwd_cos, fwd_sin)
    inputs = tokens.astype(jnp.float32)
    normed_first, unit_first, inverse_first = norm_parts(inputs, gain_first, bias_first)
    normed_first_low = normed_first.astype(jnp.bfloat16)
    query = matmul_rows(normed_first_low, query_weight)
    keyed = matmul_rows(normed_first_low, key_weight)
    valued = matmul_rows(normed_first_low, value_weight)
    shifted, keyed_spec = conv_forward(keyed, shift_spec, doc_start, tables)
    product = shifted * valued
    mixed, product_spec = conv_forward(product, long_spec, doc_start, tables)
    gated_low = (query * mixed).astype(jnp.bfloat16)
    middle = inputs + matmul_rows(gated_low, output_weight)
    normed_second, unit_second, inverse_second = norm_parts(middle, gain_second, bias_second)
    normed_second_low = normed_second.astype(jnp.bfloat16)
    hidden = matmul_rows(normed_second_low, up_weight)
    active_low = jax.nn.gelu(hidden, approximate=False).astype(jnp.bfloat16)
    layer_out = (middle + matmul_rows(active_low, down_weight)).astype(jnp.bfloat16)
    back_set = (
        lax.all_gather(owned[0], ("dp", "fsdp"), axis=0, tiled=True),
        lax.all_gather(owned[1], ("dp", "fsdp"), axis=0, tiled=True),
        lax.all_gather(owned[2], ("dp", "fsdp"), axis=0, tiled=True),
        lax.all_gather(owned[3], ("dp", "fsdp"), axis=0, tiled=True),
        lax.all_gather(owned[4], ("dp", "fsdp"), axis=0, tiled=True),
        lax.all_gather(owned[5], ("dp", "fsdp"), axis=0, tiled=True),
        lax.all_gather(owned[6], ("dp", "fsdp"), axis=0, tiled=True),
        lax.all_gather(owned[7], ("dp", "fsdp"), axis=0, tiled=True),
        lax.all_gather(owned[8], ("dp", "fsdp"), axis=0, tiled=True),
        lax.all_gather(owned[9], ("dp", "fsdp"), axis=0, tiled=True),
        lax.all_gather(owned[10], ("dp", "fsdp"), axis=0, tiled=True),
        lax.all_gather(owned[11], ("dp", "fsdp"), axis=0, tiled=True),
        lax.all_gather(owned[12], ("dp", "fsdp"), axis=0, tiled=True),
        lax.all_gather(owned[13], ("dp", "fsdp"), axis=0, tiled=True),
    )
    (
        gain_first_back,
        bias_unused_one,
        query_back,
        key_back,
        value_back,
        taps_unused,
        step_unused,
        state_unused,
        rate_unused,
        output_back,
        gain_second_back,
        bias_unused_two,
        up_back,
        down_back,
    ) = back_set
    down_grad = matmul_weight(active_low, cotangent)
    grad_active = matmul_back(cotangent, down_back)
    cumulative = 0.5 * (1.0 + lax.erf(hidden * (1.0 / math.sqrt(2.0))))
    density = jnp.exp(-0.5 * hidden * hidden) * (1.0 / math.sqrt(2.0 * math.pi))
    grad_hidden_low = (grad_active * (cumulative + hidden * density)).astype(jnp.bfloat16)
    up_grad = matmul_weight(normed_second_low, grad_hidden_low)
    grad_normed_second = matmul_back(grad_hidden_low, up_back)
    grad_middle_norm, mlp_gain_grad, mlp_bias_grad = norm_back(
        grad_normed_second, unit_second, inverse_second, gain_second_back
    )
    grad_middle = cotangent.astype(jnp.float32) + grad_middle_norm
    grad_branch_low = grad_middle.astype(jnp.bfloat16)
    output_grad = matmul_weight(gated_low, grad_branch_low)
    grad_gated = matmul_back(grad_branch_low, output_back)
    grad_query_low = (grad_gated * mixed).astype(jnp.bfloat16)
    grad_mixed = grad_gated * query
    grad_product, grad_kernel_long = conv_backward(
        grad_mixed, long_spec, product_spec, doc_start, tables
    )
    grad_shifted = grad_product * valued
    grad_value_low = (grad_product * shifted).astype(jnp.bfloat16)
    grad_keyed, grad_kernel_shift = conv_backward(
        grad_shifted, shift_spec, keyed_spec, doc_start, tables
    )
    grad_keyed_low = grad_keyed.astype(jnp.bfloat16)
    taps_grad = grad_kernel_shift[:tap_count].T
    step_grad, state_grad, rate_grad = kernel_pull(grad_kernel_long)
    query_grad = matmul_weight(normed_first_low, grad_query_low)
    key_grad = matmul_weight(normed_first_low, grad_keyed_low)
    value_grad = matmul_weight(normed_first_low, grad_value_low)
    grad_normed_first = (
        matmul_back(grad_query_low, query_back)
        + matmul_back(grad_keyed_low, key_back)
        + matmul_back(grad_value_low, value_back)
    )
    grad_inputs_norm, attn_gain_grad, attn_bias_grad = norm_back(
        grad_normed_first, unit_first, inverse_first, gain_first_back
    )
    tokens_grad = grad_middle + grad_inputs_norm
    (
        attn_gain_part,
        attn_bias_part,
        query_part,
        key_part,
        value_part,
        taps_part,
        step_part,
        state_part,
        rate_part,
        output_part,
        mlp_gain_part,
        mlp_bias_part,
        up_part,
        down_part,
    ) = (
        lax.psum_scatter(attn_gain_grad, ("dp", "fsdp"), scatter_dimension=0, tiled=True),
        lax.psum_scatter(attn_bias_grad, ("dp", "fsdp"), scatter_dimension=0, tiled=True),
        lax.psum_scatter(query_grad, ("dp", "fsdp"), scatter_dimension=0, tiled=True),
        lax.psum_scatter(key_grad, ("dp", "fsdp"), scatter_dimension=0, tiled=True),
        lax.psum_scatter(value_grad, ("dp", "fsdp"), scatter_dimension=0, tiled=True),
        lax.psum_scatter(taps_grad, ("dp", "fsdp"), scatter_dimension=0, tiled=True),
        lax.psum_scatter(step_grad, ("dp", "fsdp"), scatter_dimension=0, tiled=True),
        lax.psum_scatter(state_grad, ("dp", "fsdp"), scatter_dimension=0, tiled=True),
        lax.psum_scatter(rate_grad, ("dp", "fsdp"), scatter_dimension=0, tiled=True),
        lax.psum_scatter(output_grad, ("dp", "fsdp"), scatter_dimension=0, tiled=True),
        lax.psum_scatter(mlp_gain_grad, ("dp", "fsdp"), scatter_dimension=0, tiled=True),
        lax.psum_scatter(mlp_bias_grad, ("dp", "fsdp"), scatter_dimension=0, tiled=True),
        lax.psum_scatter(up_grad, ("dp", "fsdp"), scatter_dimension=0, tiled=True),
        lax.psum_scatter(down_grad, ("dp", "fsdp"), scatter_dimension=0, tiled=True),
    )
    return (
        layer_out,
        tokens_grad,
        attn_gain_part,
        attn_bias_part,
        query_part,
        key_part,
        value_part,
        taps_part,
        step_part,
        state_part,
        rate_part,
        output_part,
        mlp_gain_part,
        mlp_bias_part,
        up_part,
        down_part,
    )


def solution(mesh):
    placed = (
        P(("dp", "fsdp"), None),
        P(("dp", "fsdp")),
        P(("dp", "fsdp")),
        P(("dp", "fsdp")),
        P(("dp", "fsdp"), None),
        P(("dp", "fsdp"), None),
        P(("dp", "fsdp"), None),
        P(("dp", "fsdp"), None),
        P(("dp", "fsdp")),
        P(("dp", "fsdp"), None),
        P(("dp", "fsdp"), None),
        P(("dp", "fsdp"), None),
        P(("dp", "fsdp")),
        P(("dp", "fsdp")),
        P(("dp", "fsdp"), None),
        P(("dp", "fsdp"), None),
        P(("dp", "fsdp"), None),
    )
    return jax.shard_map(
        shards,
        mesh=mesh,
        in_specs=placed,
        out_specs=(
            P(("dp", "fsdp"), None),
            P(("dp", "fsdp"), None),
            P(("dp", "fsdp")),
            P(("dp", "fsdp")),
            P(("dp", "fsdp"), None),
            P(("dp", "fsdp"), None),
            P(("dp", "fsdp"), None),
            P(("dp", "fsdp"), None),
            P(("dp", "fsdp")),
            P(("dp", "fsdp"), None),
            P(("dp", "fsdp"), None),
            P(("dp", "fsdp"), None),
            P(("dp", "fsdp")),
            P(("dp", "fsdp")),
            P(("dp", "fsdp"), None),
            P(("dp", "fsdp"), None),
        ),
        check_vma=False,
    )
```

profile of v0, /device:TPU:0, one launch (start us, length us, event | category | flops | bytes accessed | tf_op | source)
XLA Modules:
  0.0 1820.4 jit_solution(9810542530599887903)
XLA Ops:
  13.5 71.2 %all_gather.56 = bf16[768,64]{1,0:T(8,128)(2,1)S(1)} all-gather(bf16[24,64]{1,0:T(8,128)(2,1)} %param.46), channel_id=1, replica_groups=mesh['dp'=4,'fsdp'=8] {'dp','fsdp'}, dimensions={0}, use_global_device_ids=true | all-gather | bytes 101376 | tf_op jit(solution)/shard_map/all_gather | solution.py:261
  90.6 37.2 %all-reduce.19 = (bf16[768]{0:T(1024)(128)(2,1)S(1)}, bf16[768]{0:T(1024)(128)(2,1)S(1)}, bf16[768]{0:T(1024)(128)(2,1)S(1)}, bf16[768]{0:T(1024)(128)(2,1)}, bf16[768]{0:T(1024)(128)(2,1)}) all-reduce(bf16[768]{0:T(1024)(128)(2,1)S(1)} %dynamic-update-slice.1, ...), channel_id=1, replica_groups=mesh['dp'=4,'fsdp'=8] {'dp','fsdp'}, use_global_device_ids=true, to_apply=%add.6 | all-reduce | flops 3840 | bytes 15360
  127.8 67.6 %all_gather.54 = bf16[768,64]{1,0:T(8,128)(2,1)S(1)} all-gather(bf16[24,64]{1,0:T(8,128)(2,1)S(1)} %copy-done.87), channel_id=1, replica_groups=mesh['dp'=4,'fsdp'=8] {'dp','fsdp'}, dimensions={0}, use_global_device_ids=true | all-gather | bytes 101376 | tf_op jit(solution)/shard_map/all_gather | solution.py:264
  195.4 64.8 %all_gather.55 = bf16[768,64]{1,0:T(8,128)(2,1)S(1)} all-gather(bf16[24,64]{1,0:T(8,128)(2,1)S(1)} %copy-done.88), channel_id=1, replica_groups=mesh['dp'=4,'fsdp'=8] {'dp','fsdp'}, dimensions={0}, use_global_device_ids=true | all-gather | bytes 101376 | tf_op jit(solution)/shard_map/all_gather | solution.py:263
  265.1 70.9 %while.124 = (s32[]{:T(128)}, f32[8,128,768]{2,1,0:T(8,128)S(1)}, f32[1,768,64]{1,2,0:T(8,128)}, f32[8]{0:T(128)S(1)}, f32[1,768,64]{1,2,0:T(8,128)}, /*index=5*/s32[]{:T(128)}) while((s32[]{:T(128)}, f32[8,128,768]{2,1,0:T(8,128)S(1)}, f32[1,768,64]{1,2,0:T(8,128)}, f32[8]{0:T(128)S(1)}, f32[1,768,64]{1,2,0:T(8,128)}, ...), condition=%wide.region_6.8_spmd.clone, body=%wide.region_4.7_spmd.clone.sunk | while | flops 18776320 | bytes 1573977 | solution.py:21
  266.6 7.5 multiply_reduce_fusion.11
  275.4 7.5 multiply_reduce_fusion.11
  284.3 7.5 multiply_reduce_fusion.11
  293.1 7.5 multiply_reduce_fusion.11
  301.9 7.5 multiply_reduce_fusion.11
  310.8 7.5 multiply_reduce_fusion.11
  319.6 7.5 multiply_reduce_fusion.11
  328.5 7.6 multiply_reduce_fusion.11
  365.2 19.4 %while.127 = (s32[]{:T(128)}, f32[8,129,768]{2,1,0:T(8,128)}, f32[8,129,768]{2,1,0:T(8,128)}, s32[8]{0:T(128)S(1)}, f32[2,129,768]{2,1,0:T(8,128)}, /*index=5*/f...) while((s32[]{:T(128)}, f32[8,129,768]{2,1,0:T(8,128)}, ...), condition=%wide.region_3.5_spmd.clone, body=%wide.region_2.4_spmd.clone.sunk | while | flops 12681250 | bytes 21399900 | solution.py:90
  376.1 8.3 select_add_fusion.15
  403.7 83.1 %while.128 = (s32[]{:T(128)}, f32[8,129,768]{2,1,0:T(8,128)}, f32[8,129,768]{2,1,0:T(8,128)}, s32[8]{0:T(128)S(1)}, f32[8,129,768]{2,1,0:T(8,128)}, /*index=5*/f...) while((s32[]{:T(128)}, f32[8,129,768]{2,1,0:T(8,128)}, ...), condition=%wide.region_8.10_spmd.clone, body=%wide.region_7.9_spmd.clone.sunk | while | flops 12681250 | bytes 21399900 | solution.py:90
  414.8 8.5 select_add_fusion.16
  425.4 8.5 select_add_fusion.16
  436.0 8.5 select_add_fusion.16
  446.5 8.5 select_add_fusion.16
  457.1 8.5 select_add_fusion.16
  467.7 8.5 select_add_fusion.16
  478.3 8.4 select_add_fusion.16
  506.9 38.5 %fusion.34 = (bf16[1024,3072]{1,0:T(8,128)(2,1)}, f32[1024,3072]{1,0:T(8,128)}) fusion(bf16[768,3072]{1,0:T(8,128)(2,1)} %all-gather.15.cloned.1.call-done, f32[1024,768]{0,1:T(8,128)} %copy-done.14, f32[768]{0:T(1024)S(1)} %copy-done.90, f32[768]{0:T(1024)S(1)} %convert_element_type.149, f32[1024]{0:T(1024)S(1)} %add_rsqrt_fusion, ...), kind=kOutput, calls=%fused_computation.95 | convolution fusion | flops 5040242688 | bytes 26753024 | tf_op jit(solution)/shard_map/dot_general | solution.py:209
  545.4 11.0 fusion.40
  582.9 84.9 %while.129 = (s32[]{:T(128)}, f32[8,129,768]{2,1,0:T(8,128)}, f32[8,129,768]{2,1,0:T(8,128)}, s32[8]{0:T(128)S(1)}, f32[8,129,768]{2,1,0:T(8,128)}, /*index=5*/f...) while((s32[]{:T(128)}, f32[8,129,768]{2,1,0:T(8,128)}, ...), condition=%wide.region_14.18_spmd.clone, body=%wide.region_13.17_spmd.clone.sunk | while | flops 12681266 | bytes 21399944 | solution.py:114
  594.3 8.5 select_add_fusion.17
  605.0 8.5 select_add_fusion.17
  615.8 8.5 select_add_fusion.17
  626.6 8.5 select_add_fusion.17
  637.4 8.5 select_add_fusion.17
  648.1 8.5 select_add_fusion.17
  658.9 8.5 select_add_fusion.17
  683.9 19.0 %while.125 = (s32[]{:T(128)}, f32[2,129,768]{2,1,0:T(8,128)}, f32[2,129,768]{2,1,0:T(8,128)}, s32[8]{0:T(128)S(1)}, f32[8,129,768]{2,1,0:T(8,128)S(1)}, /*index=...) while((s32[]{:T(128)}, f32[2,129,768]{2,1,0:T(8,128)}, ...), condition=%wide.region_29.33_spmd.clone, body=%wide.region_26.32_spmd.clone.sunk | while | flops 10897953 | bytes 27826628 | solution.py:140
  683.9 7.4 select_reduce_fusion.6
  693.3 7.6 select_reduce_fusion.6
  709.9 68.1 %while.126 = (s32[]{:T(128)}, f32[8,129,768]{2,1,0:T(8,128)}, f32[8,129,768]{2,1,0:T(8,128)}, s32[8]{0:T(128)S(1)}, f32[8,129,768]{2,1,0:T(8,128)}, /*index=5*/f...) while((s32[]{:T(128)}, f32[8,129,768]{2,1,0:T(8,128)}, ...), condition=%wide.region_34.38_spmd.clone, body=%wide.region_31.37_spmd.clone.sunk | while | flops 10897953 | bytes 15102800 | solution.py:140
  718.5 7.5 select_reduce_fusion.7
  735.4 7.5 select_reduce_fusion.7
  752.3 7.6 select_reduce_fusion.7
  760.9 7.5 select_reduce_fusion.7
  769.4 7.6 select_reduce_fusion.7
  794.4 100.9 %while.131 = (s32[]{:T(128)}, f32[768,64]{0,1:T(8,128)S(1)}, f32[768,64]{0,1:T(8,128)}, f32[8]{0:T(128)S(1)}, f32[8,128,768]{2,1,0:T(8,128)}, /*index=5*/f32[768...) while((s32[]{:T(128)}, f32[768,64]{0,1:T(8,128)S(1)}, ...), condition=%wide.region_38.42_spmd.clone, body=%wide.region_35.41_spmd.clone.sunk | while | flops 44237056 | bytes 5113031 | solution.py:21
  796.8 9.4 multiply_reduce_fusion.12
  809.4 9.4 multiply_reduce_fusion.12
  822.0 9.4 multiply_reduce_fusion.12
  834.6 9.4 multiply_reduce_fusion.12
  847.2 9.4 multiply_reduce_fusion.12
  859.8 9.4 multiply_reduce_fusion.12
  872.4 9.4 multiply_reduce_fusion.12
  885.0 9.4 multiply_reduce_fusion.12
  904.2 19.7 %while.130 = (s32[]{:T(128)}, f32[8,129,768]{2,1,0:T(8,128)}, f32[8,129,768]{2,1,0:T(8,128)}, s32[8]{0:T(128)S(1)}, f32[2,129,768]{2,1,0:T(8,128)}, /*index=5*/f...) while((s32[]{:T(128)}, f32[8,129,768]{2,1,0:T(8,128)}, ...), condition=%wide.region_16.20_spmd.clone, body=%wide.region_15.19_spmd.clone.sunk | while | flops 12681266 | bytes 21399944 | solution.py:114
  915.4 8.4 select_add_fusion.18
  942.0 10.5 fusion.140
  954.0 10.2 fusion.151
  973.5 38.2 %all-reduce.18 = (f32[768]{0:T(1024)S(1)}, f32[768]{0:T(1024)S(1)}, f32[768]{0:T(1024)S(1)}, f32[768]{0:T(1024)S(1)}, f32[768]{0:T(1024)S(1)}) all-reduce(f32[768]{0:T(1024)S(1)} %get-tuple-element.1402, f32[768]{0:T(1024)S(1)} %get-tuple-element.1406, ...), channel_id=2, replica_groups=mesh['dp'=4,'fsdp'=8] {'dp','fsdp'}, use_global_device_ids=true, to_apply=%region_20.24.clone | all-reduce | flops 3840 | bytes 30720
  1023.7 9.6 add_convert_fusion
  1037.5 75.6 %reduce-scatter.28.cloned.1.call-done = f32[24,64]{1,0:T(8,128)} async-done(((f32[768,64]{1,0:T(8,128)}), f32[24,64]{1,0:T(8,128)}) %reduce-scatter.28.cloned.1.call-update) | async-done | bytes 6160
  1113.1 103.8 %reduce-scatter.20.cloned.1.call-done = f32[24,768]{1,0:T(8,128)} async-done(((f32[768,768]{1,0:T(8,128)}), f32[24,768]{1,0:T(8,128)}) %reduce-scatter.20.cloned.1.call-update) | async-done | bytes 73744 | tf_op jit(solution)/shard_map/reduce_scatter | solution.py:426
  1216.9 104.8 %reduce-scatter.16.cloned.1.call-done = f32[24,768]{1,0:T(8,128)} async-done(((f32[768,768]{1,0:T(8,128)}), f32[24,768]{1,0:T(8,128)}) %reduce-scatter.16.cloned.1.call-update) | async-done | bytes 73744 | tf_op jit(solution)/shard_map/reduce_scatter | solution.py:420
  1321.7 103.8 %reduce-scatter.18.cloned.1.call-done = f32[24,768]{1,0:T(8,128)} async-done(((f32[768,768]{1,0:T(8,128)}), f32[24,768]{1,0:T(8,128)}) %reduce-scatter.18.cloned.1.call-update) | async-done | bytes 73744 | tf_op jit(solution)/shard_map/reduce_scatter | solution.py:421
  1425.5 104.8 %reduce-scatter.14.cloned.1.call-done = f32[24,768]{1,0:T(8,128)} async-done(((f32[768,768]{1,0:T(8,128)}), f32[24,768]{1,0:T(8,128)}) %reduce-scatter.14.cloned.1.call-update) | async-done | bytes 73744 | tf_op jit(solution)/shard_map/reduce_scatter | solution.py:419
  1530.3 141.0 %reduce-scatter.22.cloned.1.call-done = f32[24,3072]{1,0:T(8,128)} async-done(((f32[768,3072]{1,0:T(8,128)}), f32[24,3072]{1,0:T(8,128)}) %reduce-scatter.22.cloned.1.call-update) | async-done | bytes 294928 | tf_op jit(solution)/shard_map/reduce_scatter | solution.py:429
  1671.3 142.0 %reduce-scatter.24.cloned.1.call-done = f32[96,768]{1,0:T(8,128)} async-done(((f32[3072,768]{1,0:T(8,128)}), f32[96,768]{1,0:T(8,128)}) %reduce-scatter.24.cloned.1.call-update) | async-done | bytes 294928 | tf_op jit(solution)/shard_map/reduce_scatter | solution.py:430
  (551 shorter events, 344.3 us)
Async XLA Ops:
  7.2 349.9 %all-gather.9.cloned.1.call-start = ((), (), s32[]{:S(2)}) async-start(), calls=%async_computation.9 | async-start | bytes 1216512 | tf_op jit(solution)/shard_map/all_gather | solution.py:259
  7.9 385.1 %all-gather.11.cloned.1.call-start = ((), (), s32[]{:S(2)}) async-start(), calls=%async_computation.10 | async-start | bytes 1216512 | tf_op jit(solution)/shard_map/all_gather | solution.py:260
  8.7 486.6 %all-gather.7.cloned.1.call-start = ((), (), s32[]{:S(2)}) async-start(), calls=%async_computation.8 | async-start | bytes 1216512 | tf_op jit(solution)/shard_map/all_gather | solution.py:258
  9.4 492.0 %all-gather.13.cloned.1.call-start = ((), (), s32[]{:S(2)}) async-start(), calls=%async_computation.11 | async-start | bytes 1216512 | tf_op jit(solution)/shard_map/all_gather | solution.py:265
  10.0 496.9 %all-gather.15.cloned.1.call-start = ((), (), s32[]{:S(2)}) async-start(), calls=%async_computation.12 | async-start | bytes 4866048 | tf_op jit(solution)/shard_map/all_gather | solution.py:268
  10.6 534.8 %all-gather.17.cloned.1.call-start = ((), (), s32[]{:S(2)}) async-start(), calls=%async_computation.13 | async-start | bytes 4866048 | tf_op jit(solution)/shard_map/all_gather | solution.py:269
  11.1 1024.8 %all-reduce.22.cloned.1.call-start = ((), (), s32[]{:S(2)}) async-start(), calls=%async_computation.20 | async-start | bytes 393216
  85.1 5.3 copy-start.98
  85.2 42.7 %copy-start.87 = (bf16[24,64]{1,0:T(8,128)(2,1)S(1)}, bf16[24,64]{1,0:T(8,128)(2,1)}, u32[]{:S(2)}) copy-start(bf16[24,64]{1,0:T(8,128)(2,1)} %param.49) | copy-start | bytes 9220
  85.2 110.3 %copy-start.88 = (bf16[24,64]{1,0:T(8,128)(2,1)S(1)}, bf16[24,64]{1,0:T(8,128)(2,1)}, u32[]{:S(2)}) copy-start(bf16[24,64]{1,0:T(8,128)(2,1)} %param.48) | copy-start | bytes 9220
  89.4 258.7 %copy-start.82 = (f32[129]{0:T(256)}, f32[129]{0:T(256)S(1)}, u32[]{:S(2)}) copy-start(f32[129]{0:T(256)S(1)} %fusion.102) | copy-start | bytes 1552
  127.8 67.6 %copy-start.85 = (bf16[768]{0:T(1024)(128)(2,1)}, bf16[768]{0:T(1024)(128)(2,1)S(1)}, u32[]{:S(2)}) copy-start(bf16[768]{0:T(1024)(128)(2,1)S(1)} %get-tuple-element.1534) | copy-start | bytes 4612
  127.8 133.6 %copy-start.80 = (f32[768]{0:T(1024)}, f32[768]{0:T(1024)S(1)}, u32[]{:S(2)}) copy-start(f32[768]{0:T(1024)S(1)} %convert_exponential_fusion.1) | copy-start | bytes 9220
  195.4 64.8 %copy-start.33 = (bf16[768,64]{1,0:T(8,128)(2,1)}, bf16[768,64]{1,0:T(8,128)(2,1)S(1)}, u32[]{:S(2)}) copy-start(bf16[768,64]{1,0:T(8,128)(2,1)S(1)} %all_gather.54) | copy-start | bytes 294916
  344.5 6.9 copy-start.42
  344.6 11.2 copy-start.72
  347.3 8.4 copy-start.11
  347.6 9.4 copy-start.68
  348.1 8.9 copy-start.74
  350.1 221.0 %copy-start.76 = (f32[768]{0:T(1024)}, f32[768]{0:T(1024)S(1)}, u32[]{:S(2)}) copy-start(f32[768]{0:T(1024)S(1)} %convert_element_type.149) | copy-start | bytes 9220
  365.2 19.4 %copy-start.46 = (f32[129,256]{1,0:T(8,128)S(1)}, f32[129,256]{1,0:T(8,128)}, u32[]{:S(2)}) copy-start(f32[129,256]{1,0:T(8,128)} %get-tuple-element.1576) | copy-start | bytes 396292
  384.6 8.5 copy-start
  393.0 5.9 copy-start.50
  486.8 8.5 copy-start.2
  495.3 6.1 copy-start.12
  501.4 5.5 copy-start.90
  504.8 66.3 %copy-start.70 = (f32[1024]{0:T(1024)}, f32[1024]{0:T(1024)S(1)}, u32[]{:S(2)}) copy-start(f32[1024]{0:T(1024)S(1)} %broadcast_multiply_fusion.11) | copy-start | bytes 12292
  506.8 64.3 %copy-start.78 = (f32[1024]{0:T(1024)}, f32[1024]{0:T(1024)S(1)}, u32[]{:S(2)}) copy-start(f32[1024]{0:T(1024)S(1)} %add_rsqrt_fusion) | copy-start | bytes 12292
  506.8 38.6 %copy-start.43 = (bf16[1024,768]{1,0:T(8,128)(2,1)S(1)}, bf16[1024,768]{1,0:T(8,128)(2,1)}, u32[]{:S(2)}) copy-start(bf16[1024,768]{1,0:T(8,128)(2,1)} %param.55) | copy-start | bytes 4718596
  545.4 11.0 copy-start.92
  556.4 7.3 copy-start.102
  572.2 5.9 copy-start.20
  582.9 84.9 %copy-start.47 = (f32[129,256]{1,0:T(8,128)S(1)}, f32[129,256]{1,0:T(8,128)}, u32[]{:S(2)}) copy-start(f32[129,256]{1,0:T(8,128)} %get-tuple-element.1576) | copy-start | bytes 396292
  667.8 6.8 copy-start.5
  683.9 19.0 %copy-start.83 = (f32[129]{0:T(256)S(1)}, f32[129]{0:T(256)}, u32[]{:S(2)}) copy-start(f32[129]{0:T(256)} %copy-done.82) | copy-start | bytes 1552
  683.9 7.4 copy-start.64
  683.9 7.4 copy-start.66
  693.3 7.6 copy-start.64
  693.3 7.6 copy-start.66
  778.0 5.5 copy-start.32
  790.2 247.3 %reduce-scatter.26.cloned.1.call-start = ((), (), s32[]{:S(2)}) async-start(), calls=%async_computation.21 | async-start | bytes 405504
  794.4 102.2 %copy-start.34 = (bf16[768,64]{1,0:T(8,128)(2,1)S(1)}, bf16[768,64]{1,0:T(8,128)(2,1)}, u32[]{:S(2)}) copy-start(bf16[768,64]{1,0:T(8,128)(2,1)} %copy-done.33) | copy-start | bytes 294916
  794.4 102.2 %copy-start.36 = (bf16[768,64]{1,0:T(8,128)(2,1)S(1)}, bf16[768,64]{1,0:T(8,128)(2,1)}, u32[]{:S(2)}) copy-start(bf16[768,64]{1,0:T(8,128)(2,1)} %copy-done.35) | copy-start | bytes 294916
  794.4 102.2 %copy-start.81 = (f32[768]{0:T(1024)S(1)}, f32[768]{0:T(1024)}, u32[]{:S(2)}) copy-start(f32[768]{0:T(1024)} %copy-done.80) | copy-start | bytes 9220
  796.8 9.5 copy-start.27
  809.4 9.5 copy-start.27
  822.0 9.5 copy-start.27
  834.6 9.5 copy-start.27
  847.2 9.5 copy-start.27
  859.8 9.5 copy-start.27
  872.4 9.5 copy-start.27
  885.0 9.5 copy-start.27
  897.7 215.4 %reduce-scatter.28.cloned.1.call-start = ((), (), s32[]{:S(2)}) async-start(), calls=%async_computation.22 | async-start | bytes 405504
  898.5 5.7 copy-start.4
  898.5 318.4 %reduce-scatter.20.cloned.1.call-start = ((), (), s32[]{:S(2)}) async-start(), calls=%async_computation.17 | async-start | bytes 2433024 | tf_op jit(solution)/shard_map/reduce_scatter | solution.py:426
  904.1 417.5 %reduce-scatter.16.cloned.1.call-start = ((), (), s32[]{:S(2)}) async-start(), calls=%async_computation.15 | async-start | bytes 2433024 | tf_op jit(solution)/shard_map/reduce_scatter | solution.py:420
  904.2 19.7 %copy-start.48 = (f32[129,256]{1,0:T(8,128)S(1)}, f32[129,256]{1,0:T(8,128)}, u32[]{:S(2)}) copy-start(f32[129,256]{1,0:T(8,128)} %get-tuple-element.1576) | copy-start | bytes 396292
  933.9 491.6 %reduce-scatter.18.cloned.1.call-start = ((), (), s32[]{:S(2)}) async-start(), calls=%async_computation.16 | async-start | bytes 2433024 | tf_op jit(solution)/shard_map/reduce_scatter | solution.py:421
  936.8 593.5 %reduce-scatter.14.cloned.1.call-start = ((), (), s32[]{:S(2)}) async-start(), calls=%async_computation.14 | async-start | bytes 2433024 | tf_op jit(solution)/shard_map/reduce_scatter | solution.py:419
  936.8 5.2 copy-start.16
  936.8 5.2 copy-start.71
  936.8 5.2 copy-start.77
  941.7 729.6 %reduce-scatter.22.cloned.1.call-start = ((), (), s32[]{:S(2)}) async-start(), calls=%async_computation.18 | async-start | bytes 9732096 | tf_op jit(solution)/shard_map/reduce_scatter | solution.py:429
  952.6 860.8 %reduce-scatter.24.cloned.1.call-start = ((), (), s32[]{:S(2)}) async-start(), calls=%async_computation.19 | async-start | bytes 9732096 | tf_op jit(solution)/shard_map/reduce_scatter | solution.py:430
  (73 other events, 197.8 us)
Sparse Core Ops, SparseCore 0:
  11.0 56.9 all-gather.8
  71.0 53.2 all-gather.10
  127.3 53.3 all-gather.6
  183.5 53.3 all-gather.12
  239.8 62.4 all-gather.14
  305.1 62.4 all-gather.16
  790.4 121.0 all-reduce.21
  917.0 95.8 reduce-scatter.25
  1019.1 93.9 reduce-scatter.27
  1118.8 98.0 reduce-scatter.19
  1223.6 97.9 reduce-scatter.15
  1327.4 98.0 reduce-scatter.17
  1432.2 98.0 reduce-scatter.13
  1536.6 134.6 reduce-scatter.21
  1678.6 134.6 reduce-scatter.23
where the time goes:
time: 1830 us; the launch traced here: 1820 us
  waiting for transfers between devices  780 us (43%)
  other arithmetic  413 us (23%)
  blocking collectives  279 us (15%)
  matrix products  207 us (11%)
  local copies, waits for them, and re-layouts  122 us (7%)
    add x20, other arithmetic, add_offset(): total_imag + jnp.where(usable, part_imag, 0.0)  162 us
    reduce_scatter x1, waiting for transfers between devices, shards(): lax.psum_scatter(down_grad, ('dp', 'fsdp'), scatter_dimension=0, tiled=True)  142 us
    reduce_scatter x1, waiting for transfers between devices, shards(): lax.psum_scatter(up_grad, ('dp', 'fsdp'), scatter_dimension=0, tiled=True)  141 us
    reduce_sum x16, other arithmetic, one_block(): return jnp.sum(decays * weight[None, :, :], axis=2)  136 us
    reduce_scatter x1, waiting for transfers between devices, shards(): lax.psum_scatter(query_grad, ('dp', 'fsdp'), scatter_dimension=0, tiled=T...  105 us
    reduce_scatter x1, waiting for transfers between devices, shards(): lax.psum_scatter(key_grad, ('dp', 'fsdp'), scatter_dimension=0, tiled=True)  105 us
    reduce_scatter x1, waiting for transfers between devices, shards(): lax.psum_scatter(value_grad, ('dp', 'fsdp'), scatter_dimension=0, tiled=T...  104 us
    reduce_scatter x1, waiting for transfers between devices, shards(): lax.psum_scatter(output_grad, ('dp', 'fsdp'), scatter_dimension=0, tiled=...  104 us
  transfers between devices with their start and end apart: 15, of which 7 were waited for; matrix products, arithmetic and copies ran while one was open for 27% of the time, Pallas kernels for 0%

commit v1 on v0

--- a/solution.py
+++ b/solution.py
@@ -4,7 +4,365 @@
 import jax
 import jax.numpy as jnp
 from jax import lax
+from jax.experimental import pallas as pl
+from jax.experimental.pallas import tpu as pltpu
 from jax.sharding import PartitionSpec as P
+
+VMEM_LIMIT = 56 * 1024 * 1024
+
+ORDERS = ("aby", "bya", "yab", "aby", "bya", "yab", "aby", "bya")
+
+
+MESH = pl.DeviceIdType.MESH
+
+
+def mesh_dims(dp_size, fsdp_size):
+    inner = 8 if fsdp_size == 32 else 2
+    return {"y": dp_size // 2, "c": 2, "a": fsdp_size // inner, "b": inner}
+
+
+def kernels_fit(sizes, rows):
+    return rows % 8 == 0 and all(sizes[d] in (1, 2, 4) for d in "yab")
+
+
+class Place:
+    def __init__(self, sizes):
+        self.sizes = sizes
+        dp, fsdp = lax.axis_index("dp"), lax.axis_index("fsdp")
+        self.at = {
+            "y": dp // 2,
+            "c": dp % 2,
+            "a": fsdp // sizes["b"],
+            "b": fsdp % sizes["b"],
+        }
+
+    def device(self, dim, index):
+        at = dict(self.at)
+        at[dim] = index
+        return (at["y"] * 2 + at["c"], at["a"] * self.sizes["b"] + at["b"])
+
+    def shift(self, dim, step):
+        n = self.sizes[dim]
+        return (self.at[dim] + (step + n)) % n
+
+    def greet(self):
+        barrier = pltpu.get_barrier_semaphore()
+        count = 0
+        for dim in "ycab":
+            n = self.sizes[dim]
+            steps = () if n == 1 else (1,) if n == 2 else (1, -1)
+            for step in steps:
+                pl.semaphore_signal(
+                    barrier,
+                    inc=1,
+                    device_id=self.device(dim, self.shift(dim, step)),
+                    device_id_type=MESH,
+                )
+                count += 1
+        pl.semaphore_wait(barrier, count)
+
+    def view(self, buf, known, columns=None):
+        index = []
+        for dim in "ycab":
+            if dim in known:
+                index.append(pl.ds(known[dim], 1))
+            else:
+                index.append(pl.ds(0, self.sizes[dim]))
+        if columns is not None:
+            index += [slice(None), pl.ds(columns[0], columns[1])]
+        return buf.at[tuple(index)]
+
+
+class Links:
+    def __init__(self, send_sem, recv_sem):
+        self.send_sem, self.recv_sem, self.used = send_sem, recv_sem, 0
+
+    def copy(self, src, dst, device):
+        copy = pltpu.make_async_remote_copy(
+            src_ref=src,
+            dst_ref=dst,
+            send_sem=self.send_sem.at[self.used],
+            recv_sem=self.recv_sem.at[self.used],
+            device_id=device,
+            device_id_type=MESH,
+        )
+        self.used += 1
+        copy.start()
+        return copy
+
+
+def gather_steps(place, links, own, buf, order, local_sem):
+    sizes, at = place.sizes, place.at
+    columns = buf.shape[-1]
+    half = columns // 2
+    mine = {d: at[d] for d in "ycab"}
+    local = pltpu.make_async_copy(own, buf.at[at["y"], at["c"], at["a"], at["b"]], local_sem)
+    local.start()
+    own_done = False
+    passed = []
+    other = place.device("c", 1 - at["c"])
+
+    def give(known):
+        passed.append(links.copy(place.view(buf, known), place.view(buf, known), other))
+
+    local.wait()
+    give(mine)
+    known = dict(mine)
+    for dim in order:
+        n = sizes[dim]
+        if n == 1:
+            known.pop(dim)
+            continue
+        if n == 2:
+            copy = links.copy(
+                place.view(buf, known), place.view(buf, known), place.device(dim, 1 - at[dim])
+            )
+            yield
+            copy.wait()
+            arrived = dict(known)
+            arrived[dim] = 1 - at[dim]
+            give(arrived)
+            known.pop(dim)
+            continue
+        right, left = place.shift(dim, 1), place.shift(dim, -1)
+        to_right, to_left = place.device(dim, right), place.device(dim, left)
+        first = links.copy(place.view(buf, known), place.view(buf, known), to_right)
+        second = links.copy(place.view(buf, known), place.view(buf, known), to_left)
+        yield
+        first.wait()
+        second.wait()
+        from_left, from_right, far = dict(known), dict(known), dict(known)
+        from_left[dim], from_right[dim], far[dim] = left, right, place.shift(dim, 2)
+        third = links.copy(
+            place.view(buf, from_left, (0, half)), place.view(buf, from_left, (0, half)), to_right
+        )
+        fourth = links.copy(
+            place.view(buf, from_right, (half, half)),
+            place.view(buf, from_right, (half, half)),
+            to_left,
+        )
+        give(from_left)
+        give(from_right)
+        yield
+        third.wait()
+        fourth.wait()
+        give(far)
+        known.pop(dim)
+    yield
+    for copy in passed:
+        copy.wait()
+
+
+def run_all(steps):
+    active = list(steps)
+    while active:
+        left = []
+        for step in active:
+            if next(step, StopIteration) is not StopIteration:
+                left.append(step)
+        active = left
+
+
+GATHER_COPIES = 12
+
+
+def gather_kernel(sizes, orders, *refs):
+    count = len(orders)
+    owns, bufs = refs[:count], refs[count : 2 * count]
+    send_sem, recv_sem, local_sem = refs[2 * count :]
+    place = Place(sizes)
+    place.greet()
+    links = Links(send_sem, recv_sem)
+    run_all(
+        gather_steps(place, links, owns[i], bufs[i], orders[i], local_sem.at[i])
+        for i in range(count)
+    )
+
+
+def gather_all(sizes, arrays, orders, collective_id):
+    count = len(arrays)
+    lead = (sizes["y"], 2, sizes["a"], sizes["b"])
+    total = GATHER_COPIES * count
+    moved = sum(a.size for a in arrays) * 2 * math.prod(lead)
+    bufs = pl.pallas_call(
+        partial(gather_kernel, sizes, orders),
+        out_shape=[jax.ShapeDtypeStruct(lead + a.shape, a.dtype) for a in arrays],
+        in_specs=[pl.BlockSpec(memory_space=pl.ANY)] * count,
+        out_specs=[pl.BlockSpec(memory_space=pl.ANY)] * count,
+        scratch_shapes=[
+            pltpu.SemaphoreType.DMA((total,)),
+            pltpu.SemaphoreType.DMA((total,)),
+            pltpu.SemaphoreType.DMA((count,)),
+        ],
+        compiler_params=pltpu.CompilerParams(collective_id=collective_id, has_side_effects=True),
+        cost_estimate=pl.CostEstimate(flops=0, bytes_accessed=moved, transcendentals=0),
+    )(*arrays)
+    return [b.reshape((-1,) + b.shape[5:]) for b in bufs]
+
+
+def add_into(total, more, out=None):
+    lead = total.shape[:-2]
+    for flat in range(math.prod(lead)):
+        index = []
+        rest = flat
+        for n in reversed(lead):
+            index.append(rest % n)
+            rest //= n
+        index = tuple(reversed(index))
+        target = total if out is None else out
+        value = total[index].astype(jnp.float32) + more[index].astype(jnp.float32)
+        target[index] = value.astype(target.dtype)
+
+
+def add_many(total, more):
+    lead = total.shape[:-2]
+
+    def one(flat, _):
+        index = []
+        rest = flat
+        for n in reversed(lead):
+            index.append(rest % n)
+            rest = rest // n
+        index = tuple(reversed(index))
+        total[index] = (total[index].astype(jnp.float32) + more[index].astype(jnp.float32)).astype(
+            total.dtype
+        )
+        return 0
+
+    lax.fori_loop(0, math.prod(lead), one, 0)
+
+
+def scatter_steps(place, links, part, total, core_in, slots, out, order, local_sem):
+    sizes, at = place.sizes, place.at
+    half = part.shape[-1] // 2
+    local = pltpu.make_async_copy(part.at[:, at["c"]], total, local_sem)
+    local.start()
+    copy = links.copy(part.at[:, 1 - at["c"]], core_in, place.device("c", 1 - at["c"]))
+    yield
+    local.wait()
+    copy.wait()
+    add_many(total, core_in)
+    known = {}
+
+    def view(values, columns=None):
+        index = []
+        for dim in "yab":
+            index.append(
+                pl.ds(values[dim], 1) if dim in values else pl.ds(0, sizes[dim])
+            )
+        if columns is not None:
+            index += [slice(None), pl.ds(columns[0], columns[1])]
+        return total.at[tuple(index)]
+
+    slots = list(slots)
+    for dim in order:
+        n = sizes[dim]
+        here = dict(known)
+        here[dim] = at[dim]
+        if n == 2:
+            there = dict(known)
+            there[dim] = 1 - at[dim]
+            slot = slots.pop(0)
+            copy = links.copy(view(there), slot, place.device(dim, 1 - at[dim]))
+            yield
+            copy.wait()
+            add_many(view(here), slot)
+        elif n == 4:
+            right, left = place.shift(dim, 1), place.shift(dim, -1)
+            to_right, to_left = place.device(dim, right), place.device(dim, left)
+            near_right, near_left, far = dict(known), dict(known), dict(known)
+            near_right[dim], near_left[dim], far[dim] = right, left, place.shift(dim, 2)
+            half_a, half_b, whole_a, whole_b = slots[:4]
+            slots = slots[4:]
+            first = links.copy(view(far, (0, half)), half_a, to_right)
+            second = links.copy(view(far, (half, half)), half_b, to_left)
+            yield
+            first.wait()
+            second.wait()
+            add_many(view(near_right, (0, half)), half_a)
+            add_many(view(near_left, (half, half)), half_b)
+            third = links.copy(view(near_right), whole_a, to_right)
+            fourth = links.copy(view(near_left), whole_b, to_left)
+            yield
+            third.wait()
+            fourth.wait()
+            add_many(view(here), whole_a)
+            add_many(view(here), whole_b)
+        known = here
+    yield
+    out[...] = total[at["y"], at["a"], at["b"]].astype(out.dtype)
+
+
+def slot_shapes(sizes, order, rows, columns):
+    lead = {d: sizes[d] for d in "yab"}
+    shapes = []
+    for dim in order:
+        n = lead[dim]
+        lead[dim] = 1
+        whole = (lead["y"], lead["a"], lead["b"], rows, columns)
+        split = whole[:-1] + (columns // 2,)
+        if n == 2:
+            shapes.append(whole)
+        elif n == 4:
+            shapes += [split, split, whole, whole]
+    return shapes
+
+
+SCATTER_COPIES = 7
+
+
+def scatter_kernel(sizes, orders, slot_counts, *refs):
+    count = len(orders)
+    parts, outs = refs[:count], refs[count : 2 * count]
+    rest = list(refs[2 * count :])
+    totals, core_ins = rest[:count], rest[count : 2 * count]
+    rest = rest[2 * count :]
+    slots = []
+    for n in slot_counts:
+        slots.append(rest[:n])
+        rest = rest[n:]
+    send_sem, recv_sem, local_sem = rest
+    place = Place(sizes)
+    place.greet()
+    links = Links(send_sem, recv_sem)
+    run_all(
+        scatter_steps(
+            place, links, parts[i], totals[i], core_ins[i], slots[i], outs[i], orders[i], local_sem.at[i]
+        )
+        for i in range(count)
+    )
+
+
+def scatter_all(sizes, parts, orders, collective_id):
+    count = len(parts)
+    lead = (sizes["y"], 2, sizes["a"], sizes["b"])
+    devices = math.prod(lead)
+    parts = [p.reshape(lead + (p.shape[0] // devices, p.shape[1])) for p in parts]
+    blocks = [p.shape[4:] for p in parts]
+    core_lead = (lead[0],) + lead[2:]
+    slots = [slot_shapes(sizes, o, *b) for o, b in zip(orders, blocks)]
+    total = SCATTER_COPIES * count
+    planes = [pltpu.VMEM(core_lead + b, jnp.bfloat16) for b in blocks]
+    return pl.pallas_call(
+        partial(scatter_kernel, sizes, orders, [len(s) for s in slots]),
+        out_shape=[jax.ShapeDtypeStruct(b, jnp.float32) for b in blocks],
+        in_specs=[pl.BlockSpec(memory_space=pl.ANY)] * count,
+        out_specs=[pl.BlockSpec(memory_space=pltpu.VMEM)] * count,
+        scratch_shapes=planes
+        + planes
+        + [pltpu.VMEM(s, jnp.bfloat16) for group in slots for s in group]
+        + [
+            pltpu.SemaphoreType.DMA((total,)),
+            pltpu.SemaphoreType.DMA((total,)),
+            pltpu.SemaphoreType.DMA((count,)),
+        ],
+        compiler_params=pltpu.CompilerParams(
+            collective_id=collective_id, has_side_effects=True, vmem_limit_bytes=VMEM_LIMIT
+        ),
+        cost_estimate=pl.CostEstimate(
+            flops=0, bytes_accessed=sum(p.size for p in parts) * 2, transcendentals=0
+        ),
+    )(*parts)
 
 
 def make_kernel(log_step, state_out, log_rate, blocks, length):
@@ -236,58 +594,43 @@
     w_down,
     cotangent,
 ):
-    owned = (
-        attn_gain,
-        attn_bias,
-        w_query,
-        w_key,
-        w_value,
-        shift_taps,
-        log_step,
-        state_out,
-        log_rate,
-        w_output,
-        mlp_gain,
-        mlp_bias,
-        w_up,
-        w_down,
-    )
-    gathered = (
-        lax.all_gather(owned[0], ("dp", "fsdp"), axis=0, tiled=True),
-        lax.all_gather(owned[1], ("dp", "fsdp"), axis=0, tiled=True),
-        lax.all_gather(owned[2], ("dp", "fsdp"), axis=0, tiled=True),
-        lax.all_gather(owned[3], ("dp", "fsdp"), axis=0, tiled=True),
-        lax.all_gather(owned[4], ("dp", "fsdp"), axis=0, tiled=True),
-        lax.all_gather(owned[5], ("dp", "fsdp"), axis=0, tiled=True),
-        lax.all_gather(owned[6], ("dp", "fsdp"), axis=0, tiled=True),
-        lax.all_gather(owned[7], ("dp", "fsdp"), axis=0, tiled=True),
-        lax.all_gather(owned[8], ("dp", "fsdp"), axis=0, tiled=True),
-        lax.all_gather(owned[9], ("dp", "fsdp"), axis=0, tiled=True),
-        lax.all_gather(owned[10], ("dp", "fsdp"), axis=0, tiled=True),
-        lax.all_gather(owned[11], ("dp", "fsdp"), axis=0, tiled=True),
-        lax.all_gather(owned[12], ("dp", "fsdp"), axis=0, tiled=True),
-        lax.all_gather(owned[13], ("dp", "fsdp"), axis=0, tiled=True),
-    )
+    sizes = mesh_dims(lax.axis_size("dp"), lax.axis_size("fsdp"))
+    fits = kernels_fit(sizes, w_query.shape[0])
+    block_count = doc_start.shape[0]
+    block_len = tokens.shape[0] // block_count
+    kernel_fn = partial(make_kernel, blocks=block_count, length=block_len)
+    own_kernel, kernel_pull = jax.vjp(
+        kernel_fn,
+        log_step.astype(jnp.float32),
+        state_out.astype(jnp.float32),
+        log_rate.astype(jnp.float32),
+    )
+    own_rows = attn_gain.shape[0]
+    tap_count = shift_taps.shape[1]
+    small = jnp.concatenate(
+        [shift_taps]
+        + [v[:, None] for v in (attn_gain, attn_bias, mlp_gain, mlp_bias)]
+        + [jnp.zeros((own_rows, 256 - 4 - tap_count), jnp.bfloat16)],
+        axis=1,
+    )
+    owned = (w_query, w_key, w_value, small, own_kernel.T.astype(jnp.bfloat16), w_output, w_up, w_down)
+    if fits:
+        gathered = gather_all(sizes, owned, ORDERS, 0)
+    else:
+        gathered = [lax.all_gather(v, ("dp", "fsdp"), axis=0, tiled=True) for v in owned]
     (
-        gain_first,
-        bias_first,
         query_weight,
         key_weight,
         value_weight,
-        taps_weight,
-        step_weight,
-        state_weight,
-        rate_weight,
+        small_all,
+        kernel_all,
         output_weight,
-        gain_second,
-        bias_second,
         up_weight,
         down_weight,
     ) = gathered
-    row_total = tokens.shape[0]
-    block_count = doc_start.shape[0]
-    block_len = row_total // block_count
-    tap_count = taps_weight.shape[1]
+    taps_weight = small_all[:, :tap_count]
+    gain_first, bias_first, gain_second, bias_second = (small_all[:, tap_count + i] for i in range(4))
+    kernel_long = kernel_all.astype(jnp.float32).T
     fwd_cos, fwd_sin, inv_cos, inv_sin = dft_tables(block_len)
     tables = (
         fwd_cos[:, :block_len],
@@ -298,13 +641,6 @@
         fwd_sin,
         inv_cos,
         inv_sin,
-    )
-    kernel_fn = partial(make_kernel, blocks=block_count, length=block_len)
-    kernel_long, kernel_pull = jax.vjp(
-        kernel_fn,
-        step_weight.astype(jnp.float32),
-        state_weight.astype(jnp.float32),
-        rate_weight.astype(jnp.float32),
     )
     kernel_shift = jnp.pad(
         taps_weight.astype(jnp.float32).T, ((0, 2 * block_len - tap_count), (0, 0))
@@ -327,52 +663,20 @@
     hidden = matmul_rows(normed_second_low, up_weight)
     active_low = jax.nn.gelu(hidden, approximate=False).astype(jnp.bfloat16)
     layer_out = (middle + matmul_rows(active_low, down_weight)).astype(jnp.bfloat16)
-    back_set = (
-        lax.all_gather(owned[0], ("dp", "fsdp"), axis=0, tiled=True),
-        lax.all_gather(owned[1], ("dp", "fsdp"), axis=0, tiled=True),
-        lax.all_gather(owned[2], ("dp", "fsdp"), axis=0, tiled=True),
-        lax.all_gather(owned[3], ("dp", "fsdp"), axis=0, tiled=True),
-        lax.all_gather(owned[4], ("dp", "fsdp"), axis=0, tiled=True),
-        lax.all_gather(owned[5], ("dp", "fsdp"), axis=0, tiled=True),
-        lax.all_gather(owned[6], ("dp", "fsdp"), axis=0, tiled=True),
-        lax.all_gather(owned[7], ("dp", "fsdp"), axis=0, tiled=True),
-        lax.all_gather(owned[8], ("dp", "fsdp"), axis=0, tiled=True),
-        lax.all_gather(owned[9], ("dp", "fsdp"), axis=0, tiled=True),
-        lax.all_gather(owned[10], ("dp", "fsdp"), axis=0, tiled=True),
-        lax.all_gather(owned[11], ("dp", "fsdp"), axis=0, tiled=True),
-        lax.all_gather(owned[12], ("dp", "fsdp"), axis=0, tiled=True),
-        lax.all_gather(owned[13], ("dp", "fsdp"), axis=0, tiled=True),
-    )
-    (
-        gain_first_back,
-        bias_unused_one,
-        query_back,
-        key_back,
-        value_back,
-        taps_unused,
-        step_unused,
-        state_unused,
-        rate_unused,
-        output_back,
-        gain_second_back,
-        bias_unused_two,
-        up_back,
-        down_back,
-    ) = back_set
     down_grad = matmul_weight(active_low, cotangent)
-    grad_active = matmul_back(cotangent, down_back)
+    grad_active = matmul_back(cotangent, down_weight)
     cumulative = 0.5 * (1.0 + lax.erf(hidden * (1.0 / math.sqrt(2.0))))
     density = jnp.exp(-0.5 * hidden * hidden) * (1.0 / math.sqrt(2.0 * math.pi))
     grad_hidden_low = (grad_active * (cumulative + hidden * density)).astype(jnp.bfloat16)
     up_grad = matmul_weight(normed_second_low, grad_hidden_low)
-    grad_normed_second = matmul_back(grad_hidden_low, up_back)
+    grad_normed_second = matmul_back(grad_hidden_low, up_weight)
     grad_middle_norm, mlp_gain_grad, mlp_bias_grad = norm_back(
-        grad_normed_second, unit_second, inverse_second, gain_second_back
+        grad_normed_second, unit_second, inverse_second, gain_second
     )
     grad_middle = cotangent.astype(jnp.float32) + grad_middle_norm
     grad_branch_low = grad_middle.astype(jnp.bfloat16)
     output_grad = matmul_weight(gated_low, grad_branch_low)
-    grad_gated = matmul_back(grad_branch_low, output_back)
+    grad_gated = matmul_back(grad_branch_low, output_weight)
     grad_query_low = (grad_gated * mixed).astype(jnp.bfloat16)
     grad_mixed = grad_gated * query
     grad_product, grad_kernel_long = conv_backward(
@@ -385,65 +689,50 @@
     )
     grad_keyed_low = grad_keyed.astype(jnp.bfloat16)
     taps_grad = grad_kernel_shift[:tap_count].T
-    step_grad, state_grad, rate_grad = kernel_pull(grad_kernel_long)
     query_grad = matmul_weight(normed_first_low, grad_query_low)
     key_grad = matmul_weight(normed_first_low, grad_keyed_low)
     value_grad = matmul_weight(normed_first_low, grad_value_low)
     grad_normed_first = (
-        matmul_back(grad_query_low, query_back)
-        + matmul_back(grad_keyed_low, key_back)
-        + matmul_back(grad_value_low, value_back)
+        matmul_back(grad_query_low, query_weight)
+        + matmul_back(grad_keyed_low, key_weight)
+        + matmul_back(grad_value_low, value_weight)
     )
     grad_inputs_norm, attn_gain_grad, attn_bias_grad = norm_back(
-        grad_normed_first, unit_first, inverse_first, gain_first_back
+        grad_normed_first, unit_first, inverse_first, gain_first
     )
     tokens_grad = grad_middle + grad_inputs_norm
-    (
-        attn_gain_part,
-        attn_bias_part,
+    small_grad = jnp.concatenate(
+        [taps_grad]
+        + [v[:, None] for v in (attn_gain_grad, attn_bias_grad, mlp_gain_grad, mlp_bias_grad)]
+        + [jnp.zeros((taps_grad.shape[0], 256 - 4 - tap_count), jnp.float32)],
+        axis=1,
+    )
+    parts = (query_grad, key_grad, value_grad, small_grad, grad_kernel_long.T, output_grad, up_grad, down_grad)
+    parts = [p.astype(jnp.bfloat16) for p in parts]
+    if fits:
+        sums = scatter_all(sizes, parts, ORDERS, 1)
+    else:
+        sums = [
+            lax.psum_scatter(p, ("dp", "fsdp"), scatter_dimension=0, tiled=True).astype(jnp.float32)
+            for p in parts
+        ]
+    query_part, key_part, value_part, small_part, kernel_part, output_part, up_part, down_part = sums
+    step_part, state_part, rate_part = kernel_pull(kernel_part.T)
+    return (
+        layer_out,
+        tokens_grad,
+        small_part[:, tap_count],
+        small_part[:, tap_count + 1],
         query_part,
         key_part,
         value_part,
-        taps_part,
+        small_part[:, :tap_count],
         step_part,
         state_part,
         rate_part,
         output_part,
-        mlp_gain_part,
-        mlp_bias_part,
-        up_part,
-        down_part,
-    ) = (
-        lax.psum_scatter(attn_gain_grad, ("dp", "fsdp"), scatter_dimension=0, tiled=True),
-        lax.psum_scatter(attn_bias_grad, ("dp", "fsdp"), scatter_dimension=0, tiled=True),
-        lax.psum_scatter(query_grad, ("dp", "fsdp"), scatter_dimension=0, tiled=True),
-        lax.psum_scatter(key_grad, ("dp", "fsdp"), scatter_dimension=0, tiled=True),
-        lax.psum_scatter(value_grad, ("dp", "fsdp"), scatter_dimension=0, tiled=True),
-        lax.psum_scatter(taps_grad, ("dp", "fsdp"), scatter_dimension=0, tiled=True),
-        lax.psum_scatter(step_grad, ("dp", "fsdp"), scatter_dimension=0, tiled=True),
-        lax.psum_scatter(state_grad, ("dp", "fsdp"), scatter_dimension=0, tiled=True),
-        lax.psum_scatter(rate_grad, ("dp", "fsdp"), scatter_dimension=0, tiled=True),
-        lax.psum_scatter(output_grad, ("dp", "fsdp"), scatter_dimension=0, tiled=True),
-        lax.psum_scatter(mlp_gain_grad, ("dp", "fsdp"), scatter_dimension=0, tiled=True),
-        lax.psum_scatter(mlp_bias_grad, ("dp", "fsdp"), scatter_dimension=0, tiled=True),
-        lax.psum_scatter(up_grad, ("dp", "fsdp"), scatter_dimension=0, tiled=True),
-        lax.psum_scatter(down_grad, ("dp", "fsdp"), scatter_dimension=0, tiled=True),
-    )
-    return (
-        layer_out,
-        tokens_grad,
-        attn_gain_part,
-        attn_bias_part,
-        query_part,
-        key_part,
-        value_part,
-        taps_part,
-        step_part,
-        state_part,
-        rate_part,
-        output_part,
-        mlp_gain_part,
-        mlp_bias_part,
+        small_part[:, tap_count + 2],
+        small_part[:, tap_count + 3],
         up_part,
         down_part,
     )

time: 1830 us -> 831 us (0.45)
  waiting for transfers between devices: 780 us -> 0 us
  blocking collectives: 279 us -> 0 us
  Pallas kernels: 0 us -> 196 us
  other arithmetic: 413 us -> 290 us
  local copies, waits for them, and re-layouts: 122 us -> 142 us
    reduce_scatter x6 -> x0, waiting for transfers between devices: 700 us -> none  [the longest x1 142 us: shards(): lax.psum_scatter(down_grad, ('dp', 'fsdp'), scatter_dimension=0, tiled=True)]
    all_gather x3 -> x0, blocking collectives: 204 us -> none  [the longest x1 71.2 us: shards(): lax.all_gather(owned[5], ('dp', 'fsdp'), axis=0, tiled=True)]
    pallas_call x0 -> x2, Pallas kernels: none -> 196 us  [the longest x1 108 us: gather_all(): pl.pallas_call(partial(gather_kernel, sizes, orders), out_shape=[jax.Shap...]
    reduce_sum x16, other arithmetic: 136 us -> 11.6 us  [one_block(): return jnp.sum(decays * weight[None, :, :], axis=2)]
    unnamed x18 -> x0, waiting for transfers between devices: 80 us -> none
    unnamed x2 -> x0, blocking collectives: 75.4 us -> none
  transfers between devices with their start and end apart: 15 -> 0, of which waited for: 7 -> 0; matrix products, arithmetic and copies ran while one was open for 27% -> 0% of each run, Pallas kernels for 0% -> 0%
where the time goes in v1:
time: 831 us; the launch traced here: 825 us
  other arithmetic  290 us (35%)
  Pallas kernels  196 us (24%)
  matrix products  192 us (23%)
  local copies, waits for them, and re-layouts  142 us (17%)
    add x20, other arithmetic, add_offset(): total_imag + jnp.where(usable, part_imag, 0.0)  165 us
    pallas_call x1, Pallas kernels, gather_all(): pl.pallas_call(partial(gather_kernel, sizes, orders), out_shape=[jax.Shap...  108 us
    pallas_call x1, Pallas kernels, scatter_all(): pl.pallas_call(partial(scatter_kernel, sizes, orders, [len(s) for s in sl...  88.3 us
    reduce_sum x10, other arithmetic, add_offset(): jnp.sum(jnp.where(usable, grad_imag * moved_real - grad_real * moved_imag...  74.4 us
    dot_general x6, matrix products, matmul_rows(): return jnp.dot(left, right, preferred_element_type=jnp.float32)  57.5 us
    dot_general x6, matrix products, matmul_back(): jnp.einsum('td,cd->tc', left, right, preferred_element_type=jnp.float32)  28.7 us
    unnamed x207, local copies, waits for them, and re-layouts  28 us
    dot_general x6, matrix products, matmul_weight(): jnp.einsum('tc,td->cd', left, right, preferred_element_type=jnp.float32)  25.3 us

profile of v1, /device:TPU:0, one launch (start us, length us, event | category | flops | bytes accessed | tf_op | source)
XLA Modules:
  0.0 825.1 jit_solution(7585915885274164805)
XLA Ops:
  2.8 14.1 %while.124 = (s32[]{:T(128)}, bf16[8,128,24]{1,2,0:T(8,128)(2,1)S(1)}, f32[1,24,64]{2,1,0:T(8,128)S(1)}, f32[8]{0:T(128)S(1)}, f32[1,24,64]{2,1,0:T(8,128)S(1)}, /*index=5*/s32[]{:T(128)}) while((s32[]{:T(128)}, bf16[8,128,24]{1,2,0:T(8,128)(2,1)S(1)}, f32[1,24,64]{2,1,0:T(8,128)S(1)}, f32[8]{0:T(128)S(1)}, ...), condition=%wide.region_4.5_spmd.clone, body=%wide.region_2.4_spmd.clone.sunk | while | flops 587010 | bytes 31833 | solution.py:379
  22.0 107.8 %shard_map.288 = (bf16[2,2,4,2,24,768]{5,4,3,2,1,0:T(8,128)(2,1)}, bf16[2,2,4,2,24,768]{5,4,3,2,1,0:T(8,128)(2,1)}, bf16[2,2,4,2,24,768]{5,4,3,2,1,0:T(8,128)(2,...) custom-call(bf16[24,768]{1,0:T(8,128)(2,1)} %refs_0_.1, ...), custom_call_target="tpu_custom_call" | custom-call | bytes 16121856 | tf_op jit(solution)/shard_map/pallas_call | solution.py:187
  160.4 19.8 %while.127 = (s32[]{:T(128)}, f32[8,129,768]{2,1,0:T(8,128)}, f32[8,129,768]{2,1,0:T(8,128)}, s32[8]{0:T(128)S(1)}, f32[2,129,768]{2,1,0:T(8,128)}, /*index=5*/f...) while((s32[]{:T(128)}, f32[8,129,768]{2,1,0:T(8,128)}, ...), condition=%wide.region_6.8_spmd.clone, body=%wide.region_5.7_spmd.clone.sunk | while | flops 12681250 | bytes 21399900 | solution.py:448
  162.5 6.7 select_add_fusion.15
  171.3 8.5 %select_add_fusion.15 = (f32[8,129,768]{2,1,0:T(8,128)}, f32[8,129,768]{2,1,0:T(8,128)}) fusion(f32[8,129,768]{2,1,0:T(8,128)} %get-tuple-element.2098, f32[129,768]{1,0:T(8,128)} %get-tuple-element.2010, f32[129,768]{1,0:T(8,128)} %get-tuple-element.2011, pred[8]{0:T(512)(128)(4,1)S(1)} %fusion.210, pred[]{:T(512)S(6)} %compare.24, ...), kind=kLoop, calls=%fused_computation.40.clone.1 | loop fusion | flops 12681216 | bytes 19814412 | tf_op jit(solution)/shard_map/while/body/eval_jaxpr/add | solution.py:444
  180.8 4.3 fusion.100
  202.7 3.7 copy.100
  206.4 7.0 negate_bitcast_fusion.3
  213.4 4.1 fusion.68
  217.5 83.6 %while.128 = (s32[]{:T(128)}, f32[8,129,768]{2,1,0:T(8,128)}, f32[8,129,768]{2,1,0:T(8,128)}, s32[8]{0:T(128)S(1)}, f32[8,129,768]{2,1,0:T(8,128)}, /*index=5*/f...) while((s32[]{:T(128)}, f32[8,129,768]{2,1,0:T(8,128)}, ...), condition=%wide.region_8.10_spmd.clone, body=%wide.region_7.9_spmd.clone.sunk | while | flops 12681250 | bytes 21399900 | solution.py:448
  219.5 6.8 select_add_fusion.16
  228.4 8.6 %select_add_fusion.16 = (f32[8,129,768]{2,1,0:T(8,128)}, f32[8,129,768]{2,1,0:T(8,128)}) fusion(f32[8,129,768]{2,1,0:T(8,128)} %get-tuple-element.2137, f32[129,768]{1,0:T(8,128)} %get-tuple-element.2022, f32[129,768]{1,0:T(8,128)} %get-tuple-element.2023, pred[8]{0:T(512)(128)(4,1)S(1)} %fusion.211, pred[]{:T(512)S(6)} %compare.25, ...), kind=kLoop, calls=%fused_computation.52.clone.1 | loop fusion | flops 12681216 | bytes 19814412 | tf_op jit(solution)/shard_map/while/body/eval_jaxpr/add | solution.py:444
  239.1 8.6 %select_add_fusion.16 = (f32[8,129,768]{2,1,0:T(8,128)}, f32[8,129,768]{2,1,0:T(8,128)}) fusion(f32[8,129,768]{2,1,0:T(8,128)} %get-tuple-element.2137, f32[129,768]{1,0:T(8,128)} %get-tuple-element.2022, f32[129,768]{1,0:T(8,128)} %get-tuple-element.2023, pred[8]{0:T(512)(128)(4,1)S(1)} %fusion.211, pred[]{:T(512)S(6)} %compare.25, ...), kind=kLoop, calls=%fused_computation.52.clone.1 | loop fusion | flops 12681216 | bytes 19814412 | tf_op jit(solution)/shard_map/while/body/eval_jaxpr/add | solution.py:444
  249.8 8.6 %select_add_fusion.16 = (f32[8,129,768]{2,1,0:T(8,128)}, f32[8,129,768]{2,1,0:T(8,128)}) fusion(f32[8,129,768]{2,1,0:T(8,128)} %get-tuple-element.2137, f32[129,768]{1,0:T(8,128)} %get-tuple-element.2022, f32[129,768]{1,0:T(8,128)} %get-tuple-element.2023, pred[8]{0:T(512)(128)(4,1)S(1)} %fusion.211, pred[]{:T(512)S(6)} %compare.25, ...), kind=kLoop, calls=%fused_computation.52.clone.1 | loop fusion | flops 12681216 | bytes 19814412 | tf_op jit(solution)/shard_map/while/body/eval_jaxpr/add | solution.py:444
  260.4 8.6 %select_add_fusion.16 = (f32[8,129,768]{2,1,0:T(8,128)}, f32[8,129,768]{2,1,0:T(8,128)}) fusion(f32[8,129,768]{2,1,0:T(8,128)} %get-tuple-element.2137, f32[129,768]{1,0:T(8,128)} %get-tuple-element.2022, f32[129,768]{1,0:T(8,128)} %get-tuple-element.2023, pred[8]{0:T(512)(128)(4,1)S(1)} %fusion.211, pred[]{:T(512)S(6)} %compare.25, ...), kind=kLoop, calls=%fused_computation.52.clone.1 | loop fusion | flops 12681216 | bytes 19814412 | tf_op jit(solution)/shard_map/while/body/eval_jaxpr/add | solution.py:444
  271.1 8.6 %select_add_fusion.16 = (f32[8,129,768]{2,1,0:T(8,128)}, f32[8,129,768]{2,1,0:T(8,128)}) fusion(f32[8,129,768]{2,1,0:T(8,128)} %get-tuple-element.2137, f32[129,768]{1,0:T(8,128)} %get-tuple-element.2022, f32[129,768]{1,0:T(8,128)} %get-tuple-element.2023, pred[8]{0:T(512)(128)(4,1)S(1)} %fusion.211, pred[]{:T(512)S(6)} %compare.25, ...), kind=kLoop, calls=%fused_computation.52.clone.1 | loop fusion | flops 12681216 | bytes 19814412 | tf_op jit(solution)/shard_map/while/body/eval_jaxpr/add | solution.py:444
  281.8 8.6 %select_add_fusion.16 = (f32[8,129,768]{2,1,0:T(8,128)}, f32[8,129,768]{2,1,0:T(8,128)}) fusion(f32[8,129,768]{2,1,0:T(8,128)} %get-tuple-element.2137, f32[129,768]{1,0:T(8,128)} %get-tuple-element.2022, f32[129,768]{1,0:T(8,128)} %get-tuple-element.2023, pred[8]{0:T(512)(128)(4,1)S(1)} %fusion.211, pred[]{:T(512)S(6)} %compare.25, ...), kind=kLoop, calls=%fused_computation.52.clone.1 | loop fusion | flops 12681216 | bytes 19814412 | tf_op jit(solution)/shard_map/while/body/eval_jaxpr/add | solution.py:444
  292.5 8.6 %select_add_fusion.16 = (f32[8,129,768]{2,1,0:T(8,128)}, f32[8,129,768]{2,1,0:T(8,128)}) fusion(f32[8,129,768]{2,1,0:T(8,128)} %get-tuple-element.2137, f32[129,768]{1,0:T(8,128)} %get-tuple-element.2022, f32[129,768]{1,0:T(8,128)} %get-tuple-element.2023, pred[8]{0:T(512)(128)(4,1)S(1)} %fusion.211, pred[]{:T(512)S(6)} %compare.25, ...), kind=kLoop, calls=%fused_computation.52.clone.1 | loop fusion | flops 12681216 | bytes 19814412 | tf_op jit(solution)/shard_map/while/body/eval_jaxpr/add | solution.py:444
  301.1 3.8 fusion.99
  315.4 36.6 %fusion.34 = (bf16[1024,3072]{1,0:T(8,128)(2,1)}, f32[1024,3072]{1,0:T(8,128)S(1)}) fusion(bf16[768,3072]{1,0:T(8,128)(2,1)} %bitcast.325, f32[1024,768]{0,1:T(8,128)} %copy-done.20, f32[768]{0:T(1024)S(1)} %get-tuple-element.1631, f32[768]{0:T(1024)S(1)} %get-tuple-element.1632, f32[1024]{0:T(1024)S(1)} %add_rsqrt_fusion, ...), kind=kOutput, calls=%fused_computation.95 | convolution fusion | flops 5040242688 | bytes 26753024 | tf_op jit(solution)/shard_map/dot_general | solution.py:567
  352.0 9.3 %fusion.40 = bf16[1024,3072]{1,0:T(8,128)(2,1)S(1)} fusion(f32[1024,3072]{1,0:T(8,128)S(1)} %get-tuple-element.1623, bf16[3072,768]{1,0:T(8,128)(2,1)} %bitcast.323, bf16[1024,768]{1,0:T(8,128)(2,1)S(1)} %copy-done.40), kind=kOutput, calls=%fused_computation.101 | convolution fusion | flops 4863295488 | bytes 25165824 | tf_op jit(solution)/shard_map/td,cd->tc/dot_general | solution.py:571
  361.3 7.2 convolution_convert_fusion.1
  368.5 9.7 %fusion.145 = (bf16[768]{0:T(1024)(128)(2,1)}, f32[1024,768]{1,0:T(8,128)}) fusion(bf16[1024,3072]{1,0:T(8,128)(2,1)S(1)} %fusion.40, bf16[768,3072]{1,0:T(8,128)(2,1)} %bitcast.326), kind=kOutput, calls=%fused_computation.300 | convolution fusion | flops 4832623616 | bytes 14157312 | tf_op jit(solution)/shard_map/td,cd->tc/dot_general | solution.py:571
  378.1 3.6 copy.110
  381.7 4.4 multiply_reduce_fusion.3
  388.7 4.4 multiply_add_fusion
  403.4 68.0 %while.126 = (s32[]{:T(128)}, f32[8,129,768]{2,1,0:T(8,128)}, f32[8,129,768]{2,1,0:T(8,128)}, s32[8]{0:T(128)S(1)}, f32[8,129,768]{2,1,0:T(8,128)}, /*index=5*/f...) while((s32[]{:T(128)}, f32[8,129,768]{2,1,0:T(8,128)}, ...), condition=%wide.region_30.34_spmd.clone, body=%wide.region_27.33_spmd.clone.sunk | while | flops 10897953 | bytes 15102800 | solution.py:498
  403.4 7.2 select_reduce_fusion.7
  411.6 7.5 select_reduce_fusion.7
  420.2 7.3 select_reduce_fusion.7
  428.6 7.6 select_reduce_fusion.7
  437.2 7.3 select_reduce_fusion.7
  445.5 7.6 select_reduce_fusion.7
  454.1 7.4 select_reduce_fusion.7
  462.5 7.6 select_reduce_fusion.7
  471.5 5.5 fusion.79
  477.0 3.9 subtract_bitcast_fusion
  487.9 3.6 slice.122
  500.8 85.6 %while.129 = (s32[]{:T(128)}, f32[8,129,768]{2,1,0:T(8,128)}, f32[8,129,768]{2,1,0:T(8,128)}, s32[8]{0:T(128)S(1)}, f32[8,129,768]{2,1,0:T(8,128)}, /*index=5*/f...) while((s32[]{:T(128)}, f32[8,129,768]{2,1,0:T(8,128)}, ...), condition=%wide.region_14.18_spmd.clone, body=%wide.region_13.17_spmd.clone.sunk | while | flops 12681266 | bytes 21399944 | solution.py:472
  503.1 6.8 select_add_fusion.17
  512.2 8.6 %select_add_fusion.17 = (f32[8,129,768]{2,1,0:T(8,128)}, f32[8,129,768]{2,1,0:T(8,128)}) fusion(f32[8,129,768]{2,1,0:T(8,128)} %get-tuple-element.2176, f32[129,768]{1,0:T(8,128)} %get-tuple-element.2034, f32[129,768]{1,0:T(8,128)} %get-tuple-element.2035, pred[8]{0:T(512)(128)(4,1)S(1)} %dynamic_slice.384, pred[]{:T(512)S(6)} %compare.26, ...), kind=kLoop, calls=%fused_computation.64.clone.1 | loop fusion | flops 12681216 | bytes 19814412 | tf_op jit(solution)/shard_map/while/body/eval_jaxpr/add | solution.py:468
  523.1 8.6 %select_add_fusion.17 = (f32[8,129,768]{2,1,0:T(8,128)}, f32[8,129,768]{2,1,0:T(8,128)}) fusion(f32[8,129,768]{2,1,0:T(8,128)} %get-tuple-element.2176, f32[129,768]{1,0:T(8,128)} %get-tuple-element.2034, f32[129,768]{1,0:T(8,128)} %get-tuple-element.2035, pred[8]{0:T(512)(128)(4,1)S(1)} %dynamic_slice.384, pred[]{:T(512)S(6)} %compare.26, ...), kind=kLoop, calls=%fused_computation.64.clone.1 | loop fusion | flops 12681216 | bytes 19814412 | tf_op jit(solution)/shard_map/while/body/eval_jaxpr/add | solution.py:468
  534.0 8.6 %select_add_fusion.17 = (f32[8,129,768]{2,1,0:T(8,128)}, f32[8,129,768]{2,1,0:T(8,128)}) fusion(f32[8,129,768]{2,1,0:T(8,128)} %get-tuple-element.2176, f32[129,768]{1,0:T(8,128)} %get-tuple-element.2034, f32[129,768]{1,0:T(8,128)} %get-tuple-element.2035, pred[8]{0:T(512)(128)(4,1)S(1)} %dynamic_slice.384, pred[]{:T(512)S(6)} %compare.26, ...), kind=kLoop, calls=%fused_computation.64.clone.1 | loop fusion | flops 12681216 | bytes 19814412 | tf_op jit(solution)/shard_map/while/body/eval_jaxpr/add | solution.py:468
  544.9 8.7 %select_add_fusion.17 = (f32[8,129,768]{2,1,0:T(8,128)}, f32[8,129,768]{2,1,0:T(8,128)}) fusion(f32[8,129,768]{2,1,0:T(8,128)} %get-tuple-element.2176, f32[129,768]{1,0:T(8,128)} %get-tuple-element.2034, f32[129,768]{1,0:T(8,128)} %get-tuple-element.2035, pred[8]{0:T(512)(128)(4,1)S(1)} %dynamic_slice.384, pred[]{:T(512)S(6)} %compare.26, ...), kind=kLoop, calls=%fused_computation.64.clone.1 | loop fusion | flops 12681216 | bytes 19814412 | tf_op jit(solution)/shard_map/while/body/eval_jaxpr/add | solution.py:468
  555.8 8.6 %select_add_fusion.17 = (f32[8,129,768]{2,1,0:T(8,128)}, f32[8,129,768]{2,1,0:T(8,128)}) fusion(f32[8,129,768]{2,1,0:T(8,128)} %get-tuple-element.2176, f32[129,768]{1,0:T(8,128)} %get-tuple-element.2034, f32[129,768]{1,0:T(8,128)} %get-tuple-element.2035, pred[8]{0:T(512)(128)(4,1)S(1)} %dynamic_slice.384, pred[]{:T(512)S(6)} %compare.26, ...), kind=kLoop, calls=%fused_computation.64.clone.1 | loop fusion | flops 12681216 | bytes 19814412 | tf_op jit(solution)/shard_map/while/body/eval_jaxpr/add | solution.py:468
  566.7 8.7 %select_add_fusion.17 = (f32[8,129,768]{2,1,0:T(8,128)}, f32[8,129,768]{2,1,0:T(8,128)}) fusion(f32[8,129,768]{2,1,0:T(8,128)} %get-tuple-element.2176, f32[129,768]{1,0:T(8,128)} %get-tuple-element.2034, f32[129,768]{1,0:T(8,128)} %get-tuple-element.2035, pred[8]{0:T(512)(128)(4,1)S(1)} %dynamic_slice.384, pred[]{:T(512)S(6)} %compare.26, ...), kind=kLoop, calls=%fused_computation.64.clone.1 | loop fusion | flops 12681216 | bytes 19814412 | tf_op jit(solution)/shard_map/while/body/eval_jaxpr/add | solution.py:468
  577.7 8.6 %select_add_fusion.17 = (f32[8,129,768]{2,1,0:T(8,128)}, f32[8,129,768]{2,1,0:T(8,128)}) fusion(f32[8,129,768]{2,1,0:T(8,128)} %get-tuple-element.2176, f32[129,768]{1,0:T(8,128)} %get-tuple-element.2034, f32[129,768]{1,0:T(8,128)} %get-tuple-element.2035, pred[8]{0:T(512)(128)(4,1)S(1)} %dynamic_slice.384, pred[]{:T(512)S(6)} %compare.26, ...), kind=kLoop, calls=%fused_computation.64.clone.1 | loop fusion | flops 12681216 | bytes 19814412 | tf_op jit(solution)/shard_map/while/body/eval_jaxpr/add | solution.py:468
  586.5 3.8 fusion.98
  590.4 4.5 fusion.65
  603.3 18.9 %while.125 = (s32[]{:T(128)}, f32[2,129,768]{2,1,0:T(8,128)}, f32[2,129,768]{2,1,0:T(8,128)}, s32[8]{0:T(128)S(1)}, f32[8,129,768]{2,1,0:T(8,128)S(1)}, /*index=...) while((s32[]{:T(128)}, f32[2,129,768]{2,1,0:T(8,128)}, ...), condition=%wide.region_22.26_spmd.clone, body=%wide.region_19.25_spmd.clone.sunk | while | flops 10897953 | bytes 27826628 | solution.py:498
  603.3 7.4 select_reduce_fusion.6
  612.6 7.6 select_reduce_fusion.6
  629.8 20.2 %while.130 = (s32[]{:T(128)}, f32[8,129,768]{2,1,0:T(8,128)}, f32[8,129,768]{2,1,0:T(8,128)}, s32[8]{0:T(128)S(1)}, f32[2,129,768]{2,1,0:T(8,128)}, /*index=5*/f...) while((s32[]{:T(128)}, f32[8,129,768]{2,1,0:T(8,128)}, ...), condition=%wide.region_16.20_spmd.clone, body=%wide.region_15.19_spmd.clone.sunk | while | flops 12681266 | bytes 21399944 | solution.py:472
  632.2 6.8 select_add_fusion.18
  641.3 8.7 %select_add_fusion.18 = (f32[8,129,768]{2,1,0:T(8,128)}, f32[8,129,768]{2,1,0:T(8,128)}) fusion(f32[8,129,768]{2,1,0:T(8,128)} %get-tuple-element.2215, f32[129,768]{1,0:T(8,128)} %get-tuple-element.2046, f32[129,768]{1,0:T(8,128)} %get-tuple-element.2047, pred[8]{0:T(512)(128)(4,1)S(1)} %dynamic_slice.390, pred[]{:T(512)S(6)} %compare.27, ...), kind=kLoop, calls=%fused_computation.77.clone.1 | loop fusion | flops 12681216 | bytes 19814412 | tf_op jit(solution)/shard_map/while/body/eval_jaxpr/add | solution.py:468
  650.0 3.8 fusion.97
  660.5 4.2 fusion.62
  671.4 3.9 convolution_convert_fusion.3
  680.3 6.9 convolution_convert_fusion
  687.2 88.3 %shard_map.289 = (f32[24,768]{1,0:T(8,128)}, f32[24,768]{1,0:T(8,128)}, f32[24,768]{1,0:T(8,128)}, f32[24,256]{1,0:T(8,128)}, f32[24,1024]{1,0:T(8,128)}, /*inde...) custom-call(bf16[2,2,4,2,24,768]{5,4,3,2,1,0:T(8,128)(2,1)} %bitcast.312, ...), custom_call_target="tpu_custom_call" | custom-call | bytes 16121856 | tf_op jit(solution)/shard_map/pallas_call | solution.py:346
  776.5 18.1 %while.131 = (s32[]{:T(128)}, f32[24,64]{1,0:T(8,128)S(1)}, f32[24,64]{1,0:T(8,128)S(1)}, f32[8]{0:T(128)S(1)}, f32[8,128,24]{1,0,2:T(8,128)S(1)}, /*index=5*/f3...) while((s32[]{:T(128)}, f32[24,64]{1,0:T(8,128)S(1)}, ...), condition=%wide.region_34.38_spmd.clone, body=%wide.region_31.37_spmd.clone.sunk | while | flops 1382660 | bytes 111759 | solution.py:379
  798.9 5.5 fusion.61
  804.4 3.7 copy.124
  808.1 9.9 %add_convert_fusion.1 = bf16[1024,768]{0,1:T(8,128)(2,1)} fusion(f32[1024,768]{0,1:T(8,128)S(1)} %copy-done.22, bf16[1024,3072]{1,0:T(8,128)(2,1)} %get-tuple-element.1622, bf16[3072,768]{1,0:T(8,128)(2,1)} %bitcast.324), kind=kOutput, calls=%fused_computation.163 | convolution fusion | flops 4833411072 | bytes 15728640 | tf_op jit(solution)/shard_map/dot_general | solution.py:567
  (480 shorter events, 228.4 us)
Async XLA Ops:
  0.6 131.8 %copy-start.39 = (bf16[1024,768]{1,0:T(8,128)(2,1)S(1)}, bf16[1024,768]{1,0:T(8,128)(2,1)}, u32[]{:S(2)}) copy-start(bf16[1024,768]{1,0:T(8,128)(2,1)} %param.39) | copy-start | bytes 4718596
  1.4 128.4 %copy-start.89 = (f32[24]{0:T(128)}, f32[24]{0:T(128)S(1)}, u32[]{:S(2)}) copy-start(f32[24]{0:T(128)S(1)} %convert_exponential_fusion.1) | copy-start | bytes 292
  17.0 112.8 %copy-start.96 = (f32[8]{0:T(128)}, f32[8]{0:T(128)S(1)}, u32[]{:S(2)}) copy-start(f32[8]{0:T(128)S(1)} %get-tuple-element.2396) | copy-start | bytes 100
  133.3 4.3 copy-start.12
  135.6 5.1 copy-start.15
  143.4 3.8 copy-start.34
  143.9 3.3 copy-start.50
  151.4 9.0 %copy-start.93 = (s32[8]{0:T(128)S(1)}, s32[8]{0:T(128)}, u32[]{:S(2)}) copy-start(s32[8]{0:T(128)} %param.40) | copy-start | bytes 100
  180.2 5.0 copy-start
  180.8 6.2 copy-start.54
  180.8 120.3 %copy-start.44 = (f32[129,256]{1,0:T(8,128)}, f32[129,256]{1,0:T(8,128)S(1)}, u32[]{:S(2)}) copy-start(f32[129,256]{1,0:T(8,128)S(1)} %get-tuple-element.1611) | copy-start | bytes 396292
  180.8 4.3 copy-start.4
  187.1 3.2 copy-start.8
  206.4 7.0 copy-start.23
  206.4 7.0 copy-start.24
  301.1 5.8 copy-start.94
  301.1 3.8 copy-start.5
  301.1 3.8 copy-start.55
  306.9 3.3 copy-start.10
  306.9 3.3 copy-start.13
  306.9 3.7 copy-start.61
  315.4 36.6 %copy-start.40 = (bf16[1024,768]{1,0:T(8,128)(2,1)S(1)}, bf16[1024,768]{1,0:T(8,128)(2,1)}, u32[]{:S(2)}) copy-start(bf16[1024,768]{1,0:T(8,128)(2,1)} %param.55) | copy-start | bytes 4718596
  352.0 9.3 %copy-start.21 = (f32[1024,768]{0,1:T(8,128)S(1)}, f32[1024,768]{0,1:T(8,128)}, u32[]{:S(2)}) copy-start(f32[1024,768]{0,1:T(8,128)} %copy-done.20) | copy-start | bytes 9437188
  388.7 4.5 copy-start.11
  388.7 5.2 copy-start.27
  388.7 5.5 copy-start.62
  393.2 3.8 copy-start.25
  400.2 3.2 copy-start.95
  403.4 68.0 %copy-start.82 = (f32[129]{0:T(256)S(1)}, f32[129]{0:T(256)}, u32[]{:S(2)}) copy-start(f32[129]{0:T(256)} %copy-done.81) | copy-start | bytes 1552
  471.5 5.5 copy-start.33
  494.8 3.6 copy-start.26
  494.8 3.6 copy-start.32
  500.8 85.7 %copy-start.45 = (f32[129,256]{1,0:T(8,128)S(1)}, f32[129,256]{1,0:T(8,128)}, u32[]{:S(2)}) copy-start(f32[129,256]{1,0:T(8,128)} %copy-done.44) | copy-start | bytes 396292
  586.5 3.8 copy-start.6
  586.5 3.9 copy-start.9
  590.4 4.5 copy-start.29
  600.0 3.3 copy-start.1
  603.3 7.4 copy-start.63
  603.3 7.4 copy-start.65
  612.6 7.6 copy-start.63
  612.6 7.6 copy-start.65
  624.6 5.1 copy-start.2
  650.0 3.8 copy-start.7
  650.0 3.8 copy-start.56
  660.5 6.3 copy-start.86
  660.5 7.3 copy-start.88
  660.5 10.9 %copy-start.18 = (bf16[1024,768]{0,1:T(8,128)(2,1)S(1)}, bf16[1024,768]{0,1:T(8,128)(2,1)}, u32[]{:S(2)}) copy-start(bf16[1024,768]{0,1:T(8,128)(2,1)} %copy-done.15) | copy-start | bytes 4718596
  671.4 3.9 copy-start.38
  675.4 4.9 slice-start
  687.1 89.3 %copy-start.68 = (f32[24,64]{1,0:T(8,128)S(1)}, f32[24,64]{1,0:T(8,128)}, u32[]{:S(2)}) copy-start(f32[24,64]{1,0:T(8,128)} %get-tuple-element.2322) | copy-start | bytes 18436
  687.1 89.3 %copy-start.85 = (f32[24,64]{1,0:T(8,128)S(1)}, f32[24,64]{1,0:T(8,128)}, u32[]{:S(2)}) copy-start(f32[24,64]{1,0:T(8,128)} %get-tuple-element.2323) | copy-start | bytes 18436
  687.1 89.3 %copy-start.97 = (f32[8]{0:T(128)S(1)}, f32[8]{0:T(128)}, u32[]{:S(2)}) copy-start(f32[8]{0:T(128)} %copy-done.96) | copy-start | bytes 100
  687.1 107.5 %copy-start.83 = (bf16[24,64]{1,0:T(8,128)(2,1)S(1)}, bf16[24,64]{1,0:T(8,128)(2,1)}, u32[]{:S(2)}) copy-start(bf16[24,64]{1,0:T(8,128)(2,1)} %param.48) | copy-start | bytes 9220
  687.2 107.5 %copy-start.84 = (bf16[24,64]{1,0:T(8,128)(2,1)S(1)}, bf16[24,64]{1,0:T(8,128)(2,1)}, u32[]{:S(2)}) copy-start(bf16[24,64]{1,0:T(8,128)(2,1)} %param.49) | copy-start | bytes 9220
  687.2 107.5 %copy-start.90 = (f32[24]{0:T(128)S(1)}, f32[24]{0:T(128)}, u32[]{:S(2)}) copy-start(f32[24]{0:T(128)} %copy-done.89) | copy-start | bytes 292
  687.2 108.2 %copy-start.91 = (bf16[24]{0:T(256)(128)(2,1)S(1)}, bf16[24]{0:T(256)(128)(2,1)}, u32[]{:S(2)}) copy-start(bf16[24]{0:T(256)(128)(2,1)} %param.47) | copy-start | bytes 148
  687.2 111.7 %copy-start.87 = (f32[1024]{0:T(1024)S(1)}, f32[1024]{0:T(1024)}, u32[]{:S(2)}) copy-start(f32[1024]{0:T(1024)} %get-tuple-element.1444) | copy-start | bytes 12292
  804.4 3.7 copy-start.22
  808.1 12.6 %copy-start.74 = (f32[24,768]{1,0:T(8,128)S(1)}, f32[24,768]{1,0:T(8,128)}, u32[]{:S(2)}) copy-start(f32[24,768]{1,0:T(8,128)} %get-tuple-element.2367) | copy-start | bytes 221188
  818.0 3.3 copy-start.73
  818.0 4.0 copy-start.72
  818.0 4.6 copy-start.71
  818.0 5.2 copy-start.70
  818.0 5.9 copy-start.69
  (40 other events, 77.8 us)
